TPU v7x, 32 devices: a whole 2x2x4 slice. The times are simulated.
32 devices in a mesh: rep: 2 (over y), fsdp: 16 (over z, x, core).
Axes of the slice: x: 2, y: 2, z: 4, core: 2. Of those that a mesh axis runs over, the one named last changes fastest.
Arguments:
- inputs: bfloat16 [32768, 768], P(('rep', 'fsdp')), may hold values from -6 to 6
- block_kind: int32 [64], P(('rep', 'fsdp')), may hold values from 0 to 1
- query_weight: bfloat16 [768, 768], P('fsdp'), may hold values from -0.21875 to 0.21875
- query_bias: bfloat16 [768], P('fsdp'), may hold values from -3 to 3
- key_weight: bfloat16 [768, 768], P('fsdp'), may hold values from -0.21875 to 0.21875
- value_weight: bfloat16 [768, 768], P('fsdp'), may hold values from -0.21875 to 0.21875
- value_bias: bfloat16 [768], P('fsdp'), may hold values from -0.59765625 to 0.59765625
- out_weight: bfloat16 [768, 768], P('fsdp'), may hold values from -0.875 to 0.875
- out_bias: bfloat16 [768], P('fsdp'), may hold values from -3 to 3
- attn_gain: bfloat16 [768], P('fsdp'), may hold values from 0.5 to 1.5
- attn_shift: bfloat16 [768], P('fsdp'), may hold values from -3 to 3
- up_weight: bfloat16 [768, 3072], P('fsdp'), may hold values from -0.21875 to 0.21875
- up_bias: bfloat16 [3072], P('fsdp'), may hold values from -3 to 3
- down_weight: bfloat16 [3072, 768], P('fsdp'), may hold values from -0.15625 to 0.15625
- down_bias: bfloat16 [768], P('fsdp'), may hold values from -3 to 3
- ffn_gain: bfloat16 [768], P('fsdp'), may hold values from 0.5 to 1.5
- ffn_shift: bfloat16 [768], P('fsdp'), may hold values from -3 to 3
- cotangent: bfloat16 [32768, 768], P(('rep', 'fsdp')), may hold values from -6 to 6
Outputs:
- layer_out: bfloat16 [32768, 768], P(('rep', 'fsdp'))
- input_grad: float32 [32768, 768], P(('rep', 'fsdp'))
- query_weight_grad: float32 [768, 768], P('fsdp')
- query_bias_grad: float32 [768], P('fsdp')
- key_weight_grad: float32 [768, 768], P('fsdp')
- value_weight_grad: float32 [768, 768], P('fsdp')
- value_bias_grad: float32 [768], P('fsdp')
- out_weight_grad: float32 [768, 768], P('fsdp')
- out_bias_grad: float32 [768], P('fsdp')
- attn_gain_grad: float32 [768], P('fsdp')
- attn_shift_grad: float32 [768], P('fsdp')
- up_weight_grad: float32 [768, 3072], P('fsdp')
- up_bias_grad: float32 [3072], P('fsdp')
- down_weight_grad: float32 [3072, 768], P('fsdp')
- down_bias_grad: float32 [768], P('fsdp')
- ffn_gain_grad: float32 [768], P('fsdp')
- ffn_shift_grad: float32 [768], P('fsdp')
Inputs may be any that keep to these rules, and one draw needn't show every extreme that they name: `block_kind`: 1 marks a block that holds one sequence of 512 tokens; 0 marks a block that holds 4 sequences of 128 tokens each.
All inputs are finite; a program needn't handle non-finite values.
Results may differ from a plain program's by a relative error of at most 0.017.
Values may be sent and summed in bfloat16 or wider, within the bound.
No kernel may reach another device: no remote copies, remote signals or barrier semaphores. Data moves between devices by JAX's collectives and lax.ppermute only.
A program may use at most 192 MiB of HBM per device.

v0:
```python
import jax
import jax.numpy as jnp
from jax import lax
from jax.sharding import PartitionSpec as P

D = 768
H = 12
HD = 64
LONG = 512
SHORT = 128


EPSILON = 1e-05
BLOCKED = -1e30


def project(left, right):
    return jnp.dot(left, right, preferred_element_type=jnp.float32)


def contract_rows(left, right):
    return jnp.einsum("ta,tb->ab", left, right, preferred_element_type=jnp.float32)


def project_back(grad, weight):
    return jnp.einsum("tb,ab->ta", grad, weight, preferred_element_type=jnp.float32)


def heads_view(value):
    return value.reshape(value.shape[0] // LONG, LONG, H, HD)


def normalize(value):
    centered = value - jnp.mean(value, axis=-1, keepdims=True)
    inverse = lax.rsqrt(jnp.mean(centered * centered, axis=-1, keepdims=True) + EPSILON)
    return (centered * inverse, inverse)


def norm_back(grad, normed, inverse):
    return inverse * (
        grad
        - jnp.mean(grad, axis=-1, keepdims=True)
        - normed * jnp.mean(grad * normed, axis=-1, keepdims=True)
    )


def gelu_slope(value):
    return (
        0.5 * (1.0 + lax.erf(value * 0.7071067811865476))
        + value * jnp.exp(-0.5 * value * value) * 0.3989422804014327
    )


def allowed_pairs(kind):
    place = lax.broadcasted_iota(jnp.int32, (LONG,), 0)
    segment = jnp.where(kind == 1, jnp.zeros_like(place), place // SHORT)
    return segment[:, None] == segment[None, :]


def block_scores(query, keys, kind):
    raw = jnp.einsum("qhd,khd->hqk", query, keys, preferred_element_type=jnp.float32)
    allowed = allowed_pairs(kind)[None]
    return (jnp.where(allowed, raw * HD ** (-0.5), BLOCKED), allowed)


def attend_block(pieces):
    query, keys, values, kind = pieces
    scores, allowed = block_scores(query, keys, kind)
    peak = jnp.max(scores, axis=-1, keepdims=True)
    raised = jnp.exp(scores - peak)
    total = jnp.sum(raised, axis=-1, keepdims=True)
    probs = (raised / total).astype(jnp.bfloat16)
    context = jnp.einsum("hqk,khd->qhd", probs, values, preferred_element_type=jnp.float32)
    return (context.astype(jnp.bfloat16), peak + jnp.log(total))


def attend_back(pieces):
    query, keys, values, kind, logsum, grad_context = pieces
    scores, allowed = block_scores(query, keys, kind)
    probs = jnp.exp(scores - logsum)
    grad_probs = jnp.einsum(
        "qhd,khd->hqk", grad_context, values, preferred_element_type=jnp.float32
    )
    grad_values = jnp.einsum(
        "hqk,qhd->khd", probs.astype(jnp.bfloat16), grad_context, preferred_element_type=jnp.float32
    )
    grad_scores = probs * (grad_probs - jnp.sum(probs * grad_probs, axis=-1, keepdims=True))
    grad_raw = jnp.where(allowed, grad_scores * HD ** (-0.5), 0.0).astype(jnp.bfloat16)
    grad_query = jnp.einsum("hqk,khd->qhd", grad_raw, keys, preferred_element_type=jnp.float32)
    grad_keys = jnp.einsum("hqk,qhd->khd", grad_raw, query, preferred_element_type=jnp.float32)
    return (grad_query, grad_keys, grad_values)


def layer_forward(
    inputs,
    block_kind,
    query_weight,
    query_bias,
    key_weight,
    value_weight,
    value_bias,
    out_weight,
    out_bias,
    attn_gain,
    attn_shift,
    up_weight,
    up_bias,
    down_weight,
    down_bias,
    ffn_gain,
    ffn_shift,
):
    count = inputs.shape[0]
    query = (project(inputs, query_weight) + query_bias.astype(jnp.float32)).astype(jnp.bfloat16)
    keys = project(inputs, key_weight).astype(jnp.bfloat16)
    values = (project(inputs, value_weight) + value_bias.astype(jnp.float32)).astype(jnp.bfloat16)
    context, logsum = lax.map(
        attend_block, (heads_view(query), heads_view(keys), heads_view(values), block_kind)
    )
    context = context.reshape(count, D)
    branch = project(context, out_weight) + out_bias.astype(jnp.float32)
    first_norm, first_inverse = normalize(inputs.astype(jnp.float32) + branch)
    hidden = first_norm * attn_gain.astype(jnp.float32) + attn_shift.astype(jnp.float32)
    hidden_low = hidden.astype(jnp.bfloat16)
    before = project(hidden_low, up_weight) + up_bias.astype(jnp.float32)
    active = jax.nn.gelu(before, approximate=False).astype(jnp.bfloat16)
    outer = project(active, down_weight) + down_bias.astype(jnp.float32)
    second_norm, second_inverse = normalize(hidden + outer)
    output = (second_norm * ffn_gain.astype(jnp.float32) + ffn_shift.astype(jnp.float32)).astype(
        jnp.bfloat16
    )
    saved = (
        query,
        keys,
        values,
        logsum,
        context,
        first_norm,
        first_inverse,
        hidden_low,
        before,
        active,
        second_norm,
        second_inverse,
    )
    return (output, saved)


def ffn_backward(
    cotangent,
    saved,
    query_weight,
    query_bias,
    key_weight,
    value_weight,
    value_bias,
    out_weight,
    out_bias,
    attn_gain,
    attn_shift,
    up_weight,
    up_bias,
    down_weight,
    down_bias,
    ffn_gain,
    ffn_shift,
):
    (
        query,
        keys,
        values,
        logsum,
        context,
        first_norm,
        first_inverse,
        hidden_low,
        before,
        active,
        second_norm,
        second_inverse,
    ) = saved
    grad_out = cotangent.astype(jnp.float32)
    gain_grad = jnp.sum(grad_out * second_norm, axis=0)
    shift_grad = jnp.sum(grad_out, axis=0)
    grad_ffn_sum = norm_back(grad_out * ffn_gain.astype(jnp.float32), second_norm, second_inverse)
    grad_branch = grad_ffn_sum.astype(jnp.bfloat16)
    down_grad = contract_rows(active, grad_branch)
    down_bias_grad = jnp.sum(grad_branch.astype(jnp.float32), axis=0)
    grad_active = project_back(grad_branch, down_weight)
    grad_before = (grad_active * gelu_slope(before)).astype(jnp.bfloat16)
    up_grad = contract_rows(hidden_low, grad_before)
    up_bias_grad = jnp.sum(grad_before.astype(jnp.float32), axis=0)
    grad_hidden = project_back(grad_before, up_weight) + grad_ffn_sum
    return (grad_hidden, (up_grad, up_bias_grad, down_grad, down_bias_grad, gain_grad, shift_grad))


def attn_backward(
    inputs,
    block_kind,
    grad_hidden,
    saved,
    query_weight,
    query_bias,
    key_weight,
    value_weight,
    value_bias,
    out_weight,
    out_bias,
    attn_gain,
    attn_shift,
    up_weight,
    up_bias,
    down_weight,
    down_bias,
    ffn_gain,
    ffn_shift,
):
    (
        query,
        keys,
        values,
        logsum,
        context,
        first_norm,
        first_inverse,
        hidden_low,
        before,
        active,
        second_norm,
        second_inverse,
    ) = saved
    count = inputs.shape[0]
    gain_grad = jnp.sum(grad_hidden * first_norm, axis=0)
    shift_grad = jnp.sum(grad_hidden, axis=0)
    grad_attn_sum = norm_back(
        grad_hidden * attn_gain.astype(jnp.float32), first_norm, first_inverse
    )
    grad_branch = grad_attn_sum.astype(jnp.bfloat16)
    out_grad = contract_rows(context, grad_branch)
    out_bias_grad = jnp.sum(grad_branch.astype(jnp.float32), axis=0)
    grad_context = project_back(grad_branch, out_weight).astype(jnp.bfloat16)
    grad_query, grad_keys, grad_values = lax.map(
        attend_back,
        (
            heads_view(query),
            heads_view(keys),
            heads_view(values),
            block_kind,
            logsum,
            heads_view(grad_context),
        ),
    )
    grad_query = grad_query.reshape(count, D).astype(jnp.bfloat16)
    grad_keys = grad_keys.reshape(count, D).astype(jnp.bfloat16)
    grad_values = grad_values.reshape(count, D).astype(jnp.bfloat16)
    query_grad = contract_rows(inputs, grad_query)
    query_bias_grad = jnp.sum(grad_query.astype(jnp.float32), axis=0)
    key_grad = contract_rows(inputs, grad_keys)
    value_grad = contract_rows(inputs, grad_values)
    value_bias_grad = jnp.sum(grad_values.astype(jnp.float32), axis=0)
    input_grad = (
        project_back(grad_query, query_weight)
        + project_back(grad_keys, key_weight)
        + project_back(grad_values, value_weight)
        + grad_attn_sum
    )
    return (
        input_grad,
        (
            query_grad,
            query_bias_grad,
            key_grad,
            value_grad,
            value_bias_grad,
            out_grad,
            out_bias_grad,
            gain_grad,
            shift_grad,
        ),
    )


def shards(
    inputs,
    block_kind,
    query_weight,
    query_bias,
    key_weight,
    value_weight,
    value_bias,
    out_weight,
    out_bias,
    attn_gain,
    attn_shift,
    up_weight,
    up_bias,
    down_weight,
    down_bias,
    ffn_gain,
    ffn_shift,
    cotangent,
):
    gathered = (
        lax.all_gather(query_weight, "fsdp", axis=0, tiled=True),
        lax.all_gather(query_bias, "fsdp", axis=0, tiled=True),
        lax.all_gather(key_weight, "fsdp", axis=0, tiled=True),
        lax.all_gather(value_weight, "fsdp", axis=0, tiled=True),
        lax.all_gather(value_bias, "fsdp", axis=0, tiled=True),
        lax.all_gather(out_weight, "fsdp", axis=0, tiled=True),
        lax.all_gather(out_bias, "fsdp", axis=0, tiled=True),
        lax.all_gather(attn_gain, "fsdp", axis=0, tiled=True),
        lax.all_gather(attn_shift, "fsdp", axis=0, tiled=True),
        lax.all_gather(up_weight, "fsdp", axis=0, tiled=True),
        lax.all_gather(up_bias, "fsdp", axis=0, tiled=True),
        lax.all_gather(down_weight, "fsdp", axis=0, tiled=True),
        lax.all_gather(down_bias, "fsdp", axis=0, tiled=True),
        lax.all_gather(ffn_gain, "fsdp", axis=0, tiled=True),
        lax.all_gather(ffn_shift, "fsdp", axis=0, tiled=True),
    )
    layer_out, saved = layer_forward(inputs, block_kind, *gathered)
    weights_back = (
        lax.all_gather(query_weight, "fsdp", axis=0, tiled=True),
        lax.all_gather(query_bias, "fsdp", axis=0, tiled=True),
        lax.all_gather(key_weight, "fsdp", axis=0, tiled=True),
        lax.all_gather(value_weight, "fsdp", axis=0, tiled=True),
        lax.all_gather(value_bias, "fsdp", axis=0, tiled=True),
        lax.all_gather(out_weight, "fsdp", axis=0, tiled=True),
        lax.all_gather(out_bias, "fsdp", axis=0, tiled=True),
        lax.all_gather(attn_gain, "fsdp", axis=0, tiled=True),
        lax.all_gather(attn_shift, "fsdp", axis=0, tiled=True),
        lax.all_gather(up_weight, "fsdp", axis=0, tiled=True),
        lax.all_gather(up_bias, "fsdp", axis=0, tiled=True),
        lax.all_gather(down_weight, "fsdp", axis=0, tiled=True),
        lax.all_gather(down_bias, "fsdp", axis=0, tiled=True),
        lax.all_gather(ffn_gain, "fsdp", axis=0, tiled=True),
        lax.all_gather(ffn_shift, "fsdp", axis=0, tiled=True),
    )
    grad_hidden, ffn_terms = ffn_backward(cotangent, saved, *weights_back)
    up_grad, up_bias_grad, down_grad, down_bias_grad, ffn_gain_grad, ffn_shift_grad = ffn_terms
    input_grad, attn_terms = attn_backward(inputs, block_kind, grad_hidden, saved, *weights_back)
    (
        query_grad,
        query_bias_grad,
        key_grad,
        value_grad,
        value_bias_grad,
        out_grad,
        out_bias_grad,
        attn_gain_grad,
        attn_shift_grad,
    ) = attn_terms
    summed_local = (
        lax.psum_scatter(query_grad, "fsdp", scatter_dimension=0, tiled=True),
        lax.psum_scatter(query_bias_grad, "fsdp", scatter_dimension=0, tiled=True),
        lax.psum_scatter(key_grad, "fsdp", scatter_dimension=0, tiled=True),
        lax.psum_scatter(value_grad, "fsdp", scatter_dimension=0, tiled=True),
        lax.psum_scatter(value_bias_grad, "fsdp", scatter_dimension=0, tiled=True),
        lax.psum_scatter(out_grad, "fsdp", scatter_dimension=0, tiled=True),
        lax.psum_scatter(out_bias_grad, "fsdp", scatter_dimension=0, tiled=True),
        lax.psum_scatter(attn_gain_grad, "fsdp", scatter_dimension=0, tiled=True),
        lax.psum_scatter(attn_shift_grad, "fsdp", scatter_dimension=0, tiled=True),
        lax.psum_scatter(up_grad, "fsdp", scatter_dimension=0, tiled=True),
        lax.psum_scatter(up_bias_grad, "fsdp", scatter_dimension=0, tiled=True),
        lax.psum_scatter(down_grad, "fsdp", scatter_dimension=0, tiled=True),
        lax.psum_scatter(down_bias_grad, "fsdp", scatter_dimension=0, tiled=True),
        lax.psum_scatter(ffn_gain_grad, "fsdp", scatter_dimension=0, tiled=True),
        lax.psum_scatter(ffn_shift_grad, "fsdp", scatter_dimension=0, tiled=True),
    )
    (
        sum_query,
        sum_query_bias,
        sum_key,
        sum_value,
        sum_value_bias,
        sum_out,
        sum_out_bias,
        sum_attn_gain,
        sum_attn_shift,
        sum_up,
        sum_up_bias,
        sum_down,
        sum_down_bias,
        sum_ffn_gain,
        sum_ffn_shift,
    ) = summed_local
    owned_all = (
        lax.psum(sum_query.astype(jnp.bfloat16), "rep").astype(jnp.float32),
        lax.psum(sum_query_bias.astype(jnp.bfloat16), "rep").astype(jnp.float32),
        lax.psum(sum_key.astype(jnp.bfloat16), "rep").astype(jnp.float32),
        lax.psum(sum_value.astype(jnp.bfloat16), "rep").astype(jnp.float32),
        lax.psum(sum_value_bias.astype(jnp.bfloat16), "rep").astype(jnp.float32),
        lax.psum(sum_out.astype(jnp.bfloat16), "rep").astype(jnp.float32),
        lax.psum(sum_out_bias.astype(jnp.bfloat16), "rep").astype(jnp.float32),
        lax.psum(sum_attn_gain.astype(jnp.bfloat16), "rep").astype(jnp.float32),
        lax.psum(sum_attn_shift.astype(jnp.bfloat16), "rep").astype(jnp.float32),
        lax.psum(sum_up.astype(jnp.bfloat16), "rep").astype(jnp.float32),
        lax.psum(sum_up_bias.astype(jnp.bfloat16), "rep").astype(jnp.float32),
        lax.psum(sum_down.astype(jnp.bfloat16), "rep").astype(jnp.float32),
        lax.psum(sum_down_bias.astype(jnp.bfloat16), "rep").astype(jnp.float32),
        lax.psum(sum_ffn_gain.astype(jnp.bfloat16), "rep").astype(jnp.float32),
        lax.psum(sum_ffn_shift.astype(jnp.bfloat16), "rep").astype(jnp.float32),
    )
    return (layer_out, input_grad, *owned_all)


def solution(mesh):
    placed = (
        P(("rep", "fsdp"), None),
        P(("rep", "fsdp")),
        P("fsdp", None),
        P("fsdp"),
        P("fsdp", None),
        P("fsdp", None),
        P("fsdp"),
        P("fsdp", None),
        P("fsdp"),
        P("fsdp"),
        P("fsdp"),
        P("fsdp", None),
        P("fsdp"),
        P("fsdp", None),
        P("fsdp"),
        P("fsdp"),
        P("fsdp"),
        P(("rep", "fsdp"), None),
    )
    return jax.shard_map(
        shards,
        mesh=mesh,
        in_specs=placed,
        out_specs=(
            P(("rep", "fsdp"), None),
            P(("rep", "fsdp"), None),
            P("fsdp", None),
            P("fsdp"),
            P("fsdp", None),
            P("fsdp", None),
            P("fsdp"),
            P("fsdp", None),
            P("fsdp"),
            P("fsdp"),
            P("fsdp"),
            P("fsdp", None),
            P("fsdp"),
            P("fsdp", None),
            P("fsdp"),
            P("fsdp"),
            P("fsdp"),
        ),
        check_vma=False,
    )
```

profile of v0, /device:TPU:0, one launch (start us, length us, event | category | flops | bytes accessed | tf_op | source)
XLA Modules:
  0.0 1002.9 jit_solution(6090400677764351896)
XLA Ops:
  21.5 63.3 %all-reduce.19 = (bf16[768]{0:T(1024)(128)(2,1)S(1)}, bf16[768]{0:T(1024)(128)(2,1)S(1)}, bf16[768]{0:T(1024)(128)(2,1)S(1)}, bf16[768]{0:T(1024)(128)(2,1)S(1)}...) all-reduce(bf16[768]{0:T(1024)(128)(2,1)S(1)} %dynamic-update-slice, ...), channel_id=1, replica_groups=mesh['rep'=2,'fsdp'=16] {'fsdp'}, use_global_device_ids=true, to_apply=%add.1 | all-reduce | flops 9216 | bytes 36864
  90.9 3.8 add_convert_fusion.2
  104.3 26.5 %all-gather.11.cloned.1.call-done = bf16[768,768]{1,0:T(8,128)(2,1)} async-done(((bf16[48,768]{1,0:T(8,128)(2,1)}), bf16[768,768]{1,0:T(8,128)(2,1)}) %all-gather.11.cloned.1.call-update) | async-done | bytes 1179664 | tf_op jit(solution)/shard_map/all_gather | solution.py:306
  130.9 4.3 convolution_convert_fusion.1
  141.0 23.6 %while.30 = (s32[]{:T(128)}, bf16[2,512,12,64]{1,3,2,0:T(8,128)(2,1)}, f32[2,12,512,1]{2,1,3,0:T(8,128)S(1)}, bf16[2,512,12,64]{1,3,2,0:T(8,128)(2,1)}, s32[2]{0...) while((s32[]{:T(128)}, ...), condition=%wide.region_3.4_spmd, body=%wide.region_0.3_spmd.sunk | while | flops 843708928 | bytes 42170484 | solution.py:117
  147.5 5.5 fusion.189
  159.2 5.5 fusion.189
  164.6 3.0 copy.100
  170.3 3.9 fusion.130
  176.3 48.5 %all-gather.15.cloned.1.call-done = bf16[768,3072]{1,0:T(8,128)(2,1)} async-done(((bf16[48,3072]{1,0:T(8,128)(2,1)}), bf16[768,3072]{1,0:T(8,128)(2,1)}) %all-gather.15.cloned.1.call-update) | async-done | bytes 4718608 | tf_op jit(solution)/shard_map/all_gather | solution.py:313
  224.9 50.2 %fusion.98 = (bf16[1024,3072]{1,0:T(8,128)(2,1)}, f32[1024,3072]{1,0:T(8,128)}) fusion(f32[3072]{0:T(1024)S(1)} %convert_element_type.229, bf16[768,3072]{1,0:T(8,128)(2,1)} %all-gather.15.cloned.1.call-done, f32[1024,768]{0,1:T(8,128)} %copy-done.3, f32[768]{0:T(1024)S(1)} %convert_element_type.227, f32[768]{0:T(1024)S(1)} %convert_element_type.226, ...), kind=kOutput, calls=%fused_computation.96 | convolution fusion | flops 5043388416 | bytes 26765312 | tf_op jit(solution)/shard_map/dot_general | solution.py:18
  275.1 3.7 all-gather.17.cloned.1.call-done
  278.8 9.4 fusion.131
  291.7 3.2 convert_reduce_fusion.2
  294.9 14.7 %convert_reduce_fusion = (f32[3072]{0:T(1024)}, bf16[1024,3072]{1,0:T(8,128)(2,1)}) fusion(f32[1024,3072]{1,0:T(8,128)} %get-tuple-element.430, f32[3072]{0:T(1024)S(1)} %convert_element_type.229, bf16[1024,768]{0,1:T(8,128)(2,1)S(1)} %get-tuple-element.419, bf16[3072,768]{1,0:T(8,128)(2,1)S(1)} %copy-done.42), kind=kOutput, calls=%fused_computation.103 | convolution fusion | flops 4872729600 | bytes 25190400 | tf_op jit(solution)/shard_map/tb,ab->ta/dot_general | solution.py:26
  309.6 9.7 multiply_reduce_fusion.1
  322.8 2.9 fusion.121
  325.7 4.8 convolution_convert_fusion
  333.2 3.9 reshape.261
  337.0 3.0 copy.107
  340.0 129.7 %while.31 = (s32[]{:T(128)}, bf16[2,512,12,64]{1,3,2,0:T(8,128)(2,1)}, bf16[2,512,12,64]{1,3,2,0:T(8,128)(2,1)}, bf16[2,512,12,64]{1,3,2,0:T(8,128)(2,1)}, bf16[...) while((s32[]{:T(128)}, ...), condition=%wide.region_14.15_spmd, body=%wide.region_12.14_spmd.sunk | while | flops 2101626368 | bytes 163005648 | solution.py:242
  340.2 6.4 fusion.201
  346.5 6.3 fusion.200
  355.0 20.8 %bitcast_dynamic-update-slice_fusion.10 = bf16[2,512,12,64]{1,3,2,0:T(8,128)(2,1)} fusion(bf16[2,512,12,64]{1,3,2,0:T(8,128)(2,1)} %get-tuple-element.587, s32[]{:T(128)} %get-tuple-element.585, f32[12,512,512]{1,2,0:T(8,128)} %fusion.200, f32[12,512,512]{1,2,0:T(8,128)} %fusion.201, f32[12,512]{1,0:T(8,128)S(1)} %dynamic-slice_bitcast_fusion.2, ...), kind=kOutput, calls=%fused_computation.51.clone.1 | convolution fusion | flops 440408576 | bytes 53281792 | tf_op jit(solution)/shard_map/while/body/eval_jaxpr/hqk,qhd->khd/dot_general | solution.py:90
  375.8 20.4 %bitcast_dynamic-update-slice_fusion.9 = bf16[2,512,12,64]{1,3,2,0:T(8,128)(2,1)} fusion(bf16[2,512,12,64]{1,3,2,0:T(8,128)(2,1)} %get-tuple-element.586, s32[]{:T(128)} %get-tuple-element.585, f32[12,512,512]{1,2,0:T(8,128)} %fusion.200, f32[12,512,512]{1,2,0:T(8,128)} %fusion.201, f32[12,512]{1,0:T(8,128)S(1)} %dynamic-slice_bitcast_fusion.2, ...), kind=kOutput, calls=%fused_computation.52.clone.1 | convolution fusion | flops 440408576 | bytes 53281792 | tf_op jit(solution)/shard_map/while/body/eval_jaxpr/hqk,khd->qhd/dot_general | solution.py:89
  396.2 8.8 bitcast_dynamic-update-slice_fusion.11
  405.0 6.3 fusion.201
  411.3 6.3 fusion.200
  419.8 20.7 %bitcast_dynamic-update-slice_fusion.10 = bf16[2,512,12,64]{1,3,2,0:T(8,128)(2,1)} fusion(bf16[2,512,12,64]{1,3,2,0:T(8,128)(2,1)} %get-tuple-element.587, s32[]{:T(128)} %get-tuple-element.585, f32[12,512,512]{1,2,0:T(8,128)} %fusion.200, f32[12,512,512]{1,2,0:T(8,128)} %fusion.201, f32[12,512]{1,0:T(8,128)S(1)} %dynamic-slice_bitcast_fusion.2, ...), kind=kOutput, calls=%fused_computation.51.clone.1 | convolution fusion | flops 440408576 | bytes 53281792 | tf_op jit(solution)/shard_map/while/body/eval_jaxpr/hqk,qhd->khd/dot_general | solution.py:90
  440.5 20.3 %bitcast_dynamic-update-slice_fusion.9 = bf16[2,512,12,64]{1,3,2,0:T(8,128)(2,1)} fusion(bf16[2,512,12,64]{1,3,2,0:T(8,128)(2,1)} %get-tuple-element.586, s32[]{:T(128)} %get-tuple-element.585, f32[12,512,512]{1,2,0:T(8,128)} %fusion.200, f32[12,512,512]{1,2,0:T(8,128)} %fusion.201, f32[12,512]{1,0:T(8,128)S(1)} %dynamic-slice_bitcast_fusion.2, ...), kind=kOutput, calls=%fused_computation.52.clone.1 | convolution fusion | flops 440408576 | bytes 53281792 | tf_op jit(solution)/shard_map/while/body/eval_jaxpr/hqk,khd->qhd/dot_general | solution.py:89
  460.8 8.7 bitcast_dynamic-update-slice_fusion.11
  469.8 3.1 copy.109
  482.4 2.8 convolution_bitcast_fusion.1
  485.2 3.2 copy.131
  491.8 2.8 convolution_bitcast_fusion
  494.6 3.2 copy.133
  497.9 10.7 %fusion.124 = f32[768,3072]{1,0:T(8,128)} fusion(bf16[1024,3072]{1,0:T(8,128)(2,1)} %get-tuple-element.435, f32[1024,768]{0,1:T(8,128)S(1)} %copy-done.5, f32[768]{0:T(1024)S(1)} %copy-done.38, f32[768]{0:T(1024)S(1)} %copy-done.28, f32[1024]{0:T(1024)S(1)} %copy-done.30, f32[1024]{0:T(1024)S(1)} %copy-done.25), kind=kOutput, calls=%fused_computation.176 | convolution fusion | flops 4835770368 | bytes 18888704 | tf_op jit(solution)/shard_map/ta,tb->ab/dot_general | solution.py:22
  510.1 10.2 %fusion.132 = f32[3072,768]{1,0:T(8,128)} fusion(bf16[1024,3072]{1,0:T(8,128)(2,1)} %get-tuple-element.429, bf16[1024,768]{0,1:T(8,128)(2,1)S(1)} %copy-done.23), kind=kOutput, calls=%fused_computation.181 | convolution fusion | flops 4831838208 | bytes 17301504 | tf_op jit(solution)/shard_map/ta,tb->ab/dot_general | solution.py:22
  522.3 4.5 fusion.134
  526.8 3.1 fusion.133
  531.6 8.0 reduce-scatter.19.cloned.1.call-done
  541.4 64.1 %reduce-scatter.21.cloned.1.call-done = f32[48,768]{1,0:T(8,128)} async-done(((f32[768,768]{1,0:T(8,128)}), f32[48,768]{1,0:T(8,128)}) %reduce-scatter.21.cloned.1.call-update) | async-done | bytes 147472
  607.2 64.4 %reduce-scatter.23.cloned.1.call-done = f32[48,768]{1,0:T(8,128)} async-done(((f32[768,768]{1,0:T(8,128)}), f32[48,768]{1,0:T(8,128)}) %reduce-scatter.23.cloned.1.call-update) | async-done | bytes 147472
  673.3 112.8 %reduce-scatter.15.cloned.1.call-done = f32[48,3072]{1,0:T(8,128)} async-done(((f32[768,3072]{1,0:T(8,128)}), f32[48,3072]{1,0:T(8,128)}) %reduce-scatter.15.cloned.1.call-update) | async-done | bytes 589840 | tf_op jit(solution)/shard_map/reduce_scatter | solution.py:362
  787.9 113.9 %reduce-scatter.17.cloned.1.call-done = f32[192,768]{1,0:T(8,128)} async-done(((f32[3072,768]{1,0:T(8,128)}), f32[192,768]{1,0:T(8,128)}) %reduce-scatter.17.cloned.1.call-update) | async-done | bytes 589840 | tf_op jit(solution)/shard_map/reduce_scatter | solution.py:364
  904.0 60.4 %all-reduce.18 = (bf16[768]{0:T(1024)(128)(2,1)S(1)}, bf16[768]{0:T(1024)(128)(2,1)S(1)}, bf16[768]{0:T(1024)(128)(2,1)S(1)}, bf16[768]{0:T(1024)(128)(2,1)S(1)}...) all-reduce(f32[768]{0:T(1024)S(1)} %reduce_sum.190, ...), channel_id=3, replica_groups=mesh['rep'=2,'fsdp'=16] {'fsdp'}, use_global_device_ids=true, to_apply=%region_18.19.clone | all-reduce | flops 9216 | bytes 55296
  965.0 5.0 all-reduce.20
  974.7 6.0 add_add_fusion
  (251 shorter events, 108.6 us)
Async XLA Ops:
  7.2 81.5 %copy-start.11 = (bf16[1024,768]{1,0:T(8,128)(2,1)S(1)}, bf16[1024,768]{1,0:T(8,128)(2,1)}, u32[]{:S(2)}) copy-start(bf16[1024,768]{1,0:T(8,128)(2,1)} %param.39) | copy-start | bytes 4718596
  7.2 83.7 %all-gather.7.cloned.1.call-start = ((), (), s32[]{:S(2)}) async-start(), calls=%async_computation.6 | async-start | bytes 1253376 | tf_op jit(solution)/shard_map/all_gather | solution.py:307
  7.9 91.2 %all-gather.9.cloned.1.call-start = ((), (), s32[]{:S(2)}) async-start(), calls=%async_computation.7 | async-start | bytes 1253376 | tf_op jit(solution)/shard_map/all_gather | solution.py:304
  8.7 122.2 %all-gather.11.cloned.1.call-start = ((), (), s32[]{:S(2)}) async-start(), calls=%async_computation.8 | async-start | bytes 1253376 | tf_op jit(solution)/shard_map/all_gather | solution.py:306
  9.4 160.9 %all-gather.13.cloned.1.call-start = ((), (), s32[]{:S(2)}) async-start(), calls=%async_computation.9 | async-start | bytes 1253376 | tf_op jit(solution)/shard_map/all_gather | solution.py:309
  10.0 214.9 %all-gather.15.cloned.1.call-start = ((), (), s32[]{:S(2)}) async-start(), calls=%async_computation.10 | async-start | bytes 5013504 | tf_op jit(solution)/shard_map/all_gather | solution.py:313
  10.6 268.2 %all-gather.17.cloned.1.call-start = ((), (), s32[]{:S(2)}) async-start(), calls=%async_computation.11 | async-start | bytes 5013504 | tf_op jit(solution)/shard_map/all_gather | solution.py:315
  11.2 518.8 %reduce-scatter.13.cloned.1.call-start = ((), (), s32[]{:S(2)}) async-start(), calls=%async_computation.12 | async-start | bytes 2506752 | tf_op jit(solution)/shard_map/reduce_scatter | solution.py:358
  84.8 6.2 copy-start.12
  87.5 231.8 %copy-start.27 = (f32[768]{0:T(1024)}, f32[768]{0:T(1024)S(1)}, u32[]{:S(2)}) copy-start(f32[768]{0:T(1024)S(1)} %convert_element_type.226) | copy-start | bytes 9220
  87.5 191.3 %copy-start.37 = (f32[768]{0:T(1024)}, f32[768]{0:T(1024)S(1)}, u32[]{:S(2)}) copy-start(f32[768]{0:T(1024)S(1)} %convert_element_type.227) | copy-start | bytes 9220
  136.9 4.1 copy-start.44
  174.3 145.0 %copy-start.24 = (f32[1024]{0:T(1024)}, f32[1024]{0:T(1024)S(1)}, u32[]{:S(2)}) copy-start(f32[1024]{0:T(1024)S(1)} %broadcast_multiply_fusion.5) | copy-start | bytes 12292
  176.3 143.0 %copy-start.29 = (f32[1024]{0:T(1024)}, f32[1024]{0:T(1024)S(1)}, u32[]{:S(2)}) copy-start(f32[1024]{0:T(1024)S(1)} %add_rsqrt_fusion.1) | copy-start | bytes 12292
  176.3 102.5 %copy-start.39 = (f32[768]{0:T(1024)S(1)}, f32[768]{0:T(1024)}, u32[]{:S(2)}) copy-start(f32[768]{0:T(1024)} %convert_element_type.231) | copy-start | bytes 9220
  289.7 5.2 copy-start.42
  291.7 17.9 %slice-start = ((s8[4718592]{0:T(1024)(128)(4,1)}), s8[4194304]{0:T(1024)(128)(4,1)S(1)}, s32[]{:S(2)}) async-start(s8[4718592]{0:T(1024)(128)(4,1)} %bitcast.175), calls=%async_computation.19 | async-start | bytes 8388608
  294.9 14.7 %copy-start.22 = (bf16[1024,768]{0,1:T(8,128)(2,1)}, bf16[1024,768]{0,1:T(8,128)(2,1)S(1)}, u32[]{:S(2)}) copy-start(bf16[1024,768]{0,1:T(8,128)(2,1)S(1)} %get-tuple-element.419) | copy-start | bytes 4718596
  294.9 14.7 %copy-start.4 = (f32[1024,768]{0,1:T(8,128)S(1)}, f32[1024,768]{0,1:T(8,128)}, u32[]{:S(2)}) copy-start(f32[1024,768]{0,1:T(8,128)} %copy-done.3) | copy-start | bytes 9437188
  294.9 14.7 %slice-start.1 = ((s8[4718592]{0:T(1024)(128)(4,1)}), s8[524288]{0:T(1024)(128)(4,1)S(1)}, s32[]{:S(2)}) async-start(s8[4718592]{0:T(1024)(128)(4,1)} %bitcast.175), calls=%async_computation.20 | async-start | bytes 1048576
  319.3 3.5 copy-start.19
  325.7 213.9 %reduce-scatter.19.cloned.1.call-start = ((), (), s32[]{:S(2)}) async-start(), calls=%async_computation.15 | async-start | bytes 2506752
  340.2 6.4 copy-start
  340.2 6.4 copy-start.1
  405.0 6.4 copy-start
  405.0 6.4 copy-start.1
  469.7 4.7 copy-start.14
  477.8 127.6 %reduce-scatter.21.cloned.1.call-start = ((), (), s32[]{:S(2)}) async-start(), calls=%async_computation.16 | async-start | bytes 2506752
  485.2 3.3 copy-start.8
  488.5 183.1 %reduce-scatter.23.cloned.1.call-start = ((), (), s32[]{:S(2)}) async-start(), calls=%async_computation.17 | async-start | bytes 2506752
  494.6 3.3 copy-start.5
  494.6 3.3 copy-start.25
  494.6 3.3 copy-start.28
  494.6 3.3 copy-start.30
  494.6 3.3 copy-start.38
  497.8 288.2 %reduce-scatter.15.cloned.1.call-start = ((), (), s32[]{:S(2)}) async-start(), calls=%async_computation.13 | async-start | bytes 10027008 | tf_op jit(solution)/shard_map/reduce_scatter | solution.py:362
  508.7 393.0 %reduce-scatter.17.cloned.1.call-start = ((), (), s32[]{:S(2)}) async-start(), calls=%async_computation.14 | async-start | bytes 10027008 | tf_op jit(solution)/shard_map/reduce_scatter | solution.py:364
  520.3 465.3 %all-reduce.24.cloned.1.call-start = ((), (), s32[]{:S(2)}) async-start(), calls=%async_computation.18 | async-start | bytes 2506752 | tf_op jit(solution)/shard_map/psum | solution.py:387
  522.3 4.5 copy-start.18
  522.3 4.5 copy-start.43
  529.9 373.7 %copy-start.9 = (bf16[2,512,12,64]{1,3,2,0:T(8,128)(2,1)S(1)}, bf16[2,512,12,64]{1,3,2,0:T(8,128)(2,1)}, u32[]{:S(2)}) copy-start(bf16[2,512,12,64]{1,3,2,0:T(8,128)(2,1)} %get-tuple-element.240) | copy-start | bytes 4718596
  529.9 374.1 %copy-start.32 = (f32[768]{0:T(1024)S(1)}, f32[768]{0:T(1024)}, u32[]{:S(2)}) copy-start(f32[768]{0:T(1024)} %get-tuple-element.418) | copy-start | bytes 9220
  529.9 374.1 %copy-start.33 = (f32[768]{0:T(1024)S(1)}, f32[768]{0:T(1024)}, u32[]{:S(2)}) copy-start(f32[768]{0:T(1024)} %get-tuple-element.420) | copy-start | bytes 9220
  529.9 374.1 %copy-start.34 = (f32[768]{0:T(1024)S(1)}, f32[768]{0:T(1024)}, u32[]{:S(2)}) copy-start(f32[768]{0:T(1024)} %get-tuple-element.345) | copy-start | bytes 9220
  529.9 374.1 %copy-start.35 = (f32[768]{0:T(1024)S(1)}, f32[768]{0:T(1024)}, u32[]{:S(2)}) copy-start(f32[768]{0:T(1024)} %get-tuple-element.350) | copy-start | bytes 9220
  529.9 374.1 %copy-start.36 = (f32[3072]{0:T(1024)S(1)}, f32[3072]{0:T(1024)}, u32[]{:S(2)}) copy-start(f32[3072]{0:T(1024)} %get-tuple-element.434) | copy-start | bytes 36868
  529.9 374.1 %copy-start.40 = (f32[768]{0:T(1024)S(1)}, f32[768]{0:T(1024)}, u32[]{:S(2)}) copy-start(f32[768]{0:T(1024)} %get-tuple-element.343) | copy-start | bytes 9220
  529.9 374.1 %copy-start.41 = (f32[768]{0:T(1024)S(1)}, f32[768]{0:T(1024)}, u32[]{:S(2)}) copy-start(f32[768]{0:T(1024)} %get-tuple-element.348) | copy-start | bytes 9220
  (14 other events, 24.1 us)
Sparse Core Ops, SparseCore 0:
  10.3 41.1 all-gather.6
  53.8 37.2 all-gather.8
  93.4 37.4 all-gather.10
  133.0 37.2 all-gather.12
  172.5 52.3 all-gather.14
  227.0 51.7 all-gather.16
  325.8 61.4 reduce-scatter.12
  478.0 61.6 reduce-scatter.18
  543.4 62.0 reduce-scatter.20
  609.5 61.9 reduce-scatter.22
  675.7 110.3 reduce-scatter.14
  790.6 111.1 reduce-scatter.16
  905.5 45.1 all-reduce.23
where the time goes:
time: 1010 us; the launch traced here: 1000 us
  waiting for transfers between devices  447 us (44%)
  matrix products  288 us (29%)
  blocking collectives  129 us (13%)
  local copies, waits for them, and re-layouts  84.9 us (8%)
  other arithmetic  32.7 us (3%)
  between operations  17.9 us (2%)
    unnamed x16, waiting for transfers between devices  140 us
    unnamed x2, blocking collectives  124 us
    reduce_scatter x1, waiting for transfers between devices, shards(): lax.psum_scatter(down_grad, 'fsdp', scatter_dimension=0, tiled=True)  114 us
    reduce_scatter x1, waiting for transfers between devices, shards(): lax.psum_scatter(up_grad, 'fsdp', scatter_dimension=0, tiled=True)  113 us
    dot_general x6, matrix products, project(): return jnp.dot(left, right, preferred_element_type=jnp.float32)  74.4 us
    unnamed x135, local copies, waits for them, and re-layouts  51.1 us
    all_gather x1, waiting for transfers between devices, shards(): lax.all_gather(up_weight, 'fsdp', axis=0, tiled=True)  48.5 us
    dot_general x6, matrix products, project_back(): jnp.einsum('tb,ab->ta', grad, weight, preferred_element_type=jnp.float32)  42.7 us
  transfers between devices with their start and end apart: 13, of which 9 were waited for; matrix products, arithmetic and copies ran while one was open for 34% of the time, Pallas kernels for 0%

commit v1 on v0

--- a/solution.py
+++ b/solution.py
@@ -280,6 +280,47 @@
     )
 
 
+def swap(value, mask, count):
+    return lax.ppermute(value, "fsdp", [(i, i ^ mask) for i in range(count)])
+
+
+def gather_rows(piece, count):
+    me = lax.axis_index("fsdp")
+    held = piece[None]
+    bit = count // 2
+    while bit:
+        other = swap(held, bit, count)
+        mine_low = (me & bit) == 0
+        held = jnp.stack(
+            [jnp.where(mine_low, held, other), jnp.where(mine_low, other, held)], axis=1
+        ).reshape((-1,) + piece.shape)
+        bit //= 2
+    return held
+
+
+def scatter_sum(parts, count):
+    me = lax.axis_index("fsdp")
+    held = parts
+    bit = 1
+    while bit < count:
+        pairs = held.reshape((held.shape[0] // 2, 2) + held.shape[1:])
+        mine = ((me & bit) != 0).astype(jnp.int32)
+        keep = lax.dynamic_index_in_dim(pairs, mine, 1, keepdims=False)
+        send = lax.dynamic_index_in_dim(pairs, 1 - mine, 1, keepdims=False)
+        held = (keep.astype(jnp.float32) + swap(send, bit, count).astype(jnp.float32)).astype(
+            jnp.bfloat16
+        )
+        bit *= 2
+    held = held[0]
+    other = lax.ppermute(held, "rep", [(0, 1), (1, 0)])
+    return held.astype(jnp.float32) + other.astype(jnp.float32)
+
+
+def pack_vectors(vectors, rows):
+    flat = jnp.concatenate([v.reshape(-1) for v in vectors])
+    return jnp.pad(flat, (0, rows * D - flat.shape[0])).reshape(rows, D)
+
+
 def shards(
     inputs,
     block_kind,
@@ -300,44 +341,67 @@
     ffn_shift,
     cotangent,
 ):
+    rows = query_weight.shape[0]
+    count = D // rows
+    wide = up_weight.shape[1] // D
+    vectors = (
+        query_bias,
+        value_bias,
+        out_bias,
+        attn_gain,
+        attn_shift,
+        up_bias,
+        down_bias,
+        ffn_gain,
+        ffn_shift,
+    )
+    sizes = [v.shape[0] for v in vectors]
+    spare = -(-sum(sizes) // D)
+    first = gather_rows(
+        jnp.concatenate([query_weight, key_weight, value_weight, pack_vectors(vectors, spare)]),
+        count,
+    )
+    second = gather_rows(
+        jnp.concatenate(
+            [out_weight] + [up_weight[:, D * i : D * (i + 1)] for i in range(wide)]
+        ),
+        count,
+    )
+    third = gather_rows(down_weight, count)
+    all_query = first[:, :rows].reshape(D, D)
+    all_key = first[:, rows : 2 * rows].reshape(D, D)
+    all_value = first[:, 2 * rows : 3 * rows].reshape(D, D)
+    flat = first[:, 3 * rows :].reshape(count, -1)
+    whole, at = [], 0
+    for size in sizes:
+        whole.append(flat[:, at : at + size].reshape(-1))
+        at += size
+    all_out = second[:, :rows].reshape(D, D)
+    all_up = jnp.concatenate(
+        [second[:, rows * (1 + i) : rows * (2 + i)].reshape(D, D) for i in range(wide)], axis=1
+    )
+    all_down = third.reshape(-1, D)
     gathered = (
-        lax.all_gather(query_weight, "fsdp", axis=0, tiled=True),
-        lax.all_gather(query_bias, "fsdp", axis=0, tiled=True),
-        lax.all_gather(key_weight, "fsdp", axis=0, tiled=True),
-        lax.all_gather(value_weight, "fsdp", axis=0, tiled=True),
-        lax.all_gather(value_bias, "fsdp", axis=0, tiled=True),
-        lax.all_gather(out_weight, "fsdp", axis=0, tiled=True),
-        lax.all_gather(out_bias, "fsdp", axis=0, tiled=True),
-        lax.all_gather(attn_gain, "fsdp", axis=0, tiled=True),
-        lax.all_gather(attn_shift, "fsdp", axis=0, tiled=True),
-        lax.all_gather(up_weight, "fsdp", axis=0, tiled=True),
-        lax.all_gather(up_bias, "fsdp", axis=0, tiled=True),
-        lax.all_gather(down_weight, "fsdp", axis=0, tiled=True),
-        lax.all_gather(down_bias, "fsdp", axis=0, tiled=True),
-        lax.all_gather(ffn_gain, "fsdp", axis=0, tiled=True),
-        lax.all_gather(ffn_shift, "fsdp", axis=0, tiled=True),
+        all_query,
+        whole[0],
+        all_key,
+        all_value,
+        whole[1],
+        all_out,
+        whole[2],
+        whole[3],
+        whole[4],
+        all_up,
+        whole[5],
+        all_down,
+        whole[6],
+        whole[7],
+        whole[8],
     )
     layer_out, saved = layer_forward(inputs, block_kind, *gathered)
-    weights_back = (
-        lax.all_gather(query_weight, "fsdp", axis=0, tiled=True),
-        lax.all_gather(query_bias, "fsdp", axis=0, tiled=True),
-        lax.all_gather(key_weight, "fsdp", axis=0, tiled=True),
-        lax.all_gather(value_weight, "fsdp", axis=0, tiled=True),
-        lax.all_gather(value_bias, "fsdp", axis=0, tiled=True),
-        lax.all_gather(out_weight, "fsdp", axis=0, tiled=True),
-        lax.all_gather(out_bias, "fsdp", axis=0, tiled=True),
-        lax.all_gather(attn_gain, "fsdp", axis=0, tiled=True),
-        lax.all_gather(attn_shift, "fsdp", axis=0, tiled=True),
-        lax.all_gather(up_weight, "fsdp", axis=0, tiled=True),
-        lax.all_gather(up_bias, "fsdp", axis=0, tiled=True),
-        lax.all_gather(down_weight, "fsdp", axis=0, tiled=True),
-        lax.all_gather(down_bias, "fsdp", axis=0, tiled=True),
-        lax.all_gather(ffn_gain, "fsdp", axis=0, tiled=True),
-        lax.all_gather(ffn_shift, "fsdp", axis=0, tiled=True),
-    )
-    grad_hidden, ffn_terms = ffn_backward(cotangent, saved, *weights_back)
+    grad_hidden, ffn_terms = ffn_backward(cotangent, saved, *gathered)
     up_grad, up_bias_grad, down_grad, down_bias_grad, ffn_gain_grad, ffn_shift_grad = ffn_terms
-    input_grad, attn_terms = attn_backward(inputs, block_kind, grad_hidden, saved, *weights_back)
+    input_grad, attn_terms = attn_backward(inputs, block_kind, grad_hidden, saved, *gathered)
     (
         query_grad,
         query_bias_grad,
@@ -349,58 +413,67 @@
         attn_gain_grad,
         attn_shift_grad,
     ) = attn_terms
-    summed_local = (
-        lax.psum_scatter(query_grad, "fsdp", scatter_dimension=0, tiled=True),
-        lax.psum_scatter(query_bias_grad, "fsdp", scatter_dimension=0, tiled=True),
-        lax.psum_scatter(key_grad, "fsdp", scatter_dimension=0, tiled=True),
-        lax.psum_scatter(value_grad, "fsdp", scatter_dimension=0, tiled=True),
-        lax.psum_scatter(value_bias_grad, "fsdp", scatter_dimension=0, tiled=True),
-        lax.psum_scatter(out_grad, "fsdp", scatter_dimension=0, tiled=True),
-        lax.psum_scatter(out_bias_grad, "fsdp", scatter_dimension=0, tiled=True),
-        lax.psum_scatter(attn_gain_grad, "fsdp", scatter_dimension=0, tiled=True),
-        lax.psum_scatter(attn_shift_grad, "fsdp", scatter_dimension=0, tiled=True),
-        lax.psum_scatter(up_grad, "fsdp", scatter_dimension=0, tiled=True),
-        lax.psum_scatter(up_bias_grad, "fsdp", scatter_dimension=0, tiled=True),
-        lax.psum_scatter(down_grad, "fsdp", scatter_dimension=0, tiled=True),
-        lax.psum_scatter(down_bias_grad, "fsdp", scatter_dimension=0, tiled=True),
-        lax.psum_scatter(ffn_gain_grad, "fsdp", scatter_dimension=0, tiled=True),
-        lax.psum_scatter(ffn_shift_grad, "fsdp", scatter_dimension=0, tiled=True),
-    )
-    (
-        sum_query,
-        sum_query_bias,
-        sum_key,
-        sum_value,
-        sum_value_bias,
-        sum_out,
-        sum_out_bias,
-        sum_attn_gain,
-        sum_attn_shift,
+    low = jnp.bfloat16
+    sum_down = scatter_sum(down_grad.astype(low).reshape(count, -1, D), count)
+    sum_second = scatter_sum(
+        jnp.concatenate(
+            [out_grad.astype(low).reshape(count, rows, D)]
+            + [
+                up_grad[:, D * i : D * (i + 1)].astype(low).reshape(count, rows, D)
+                for i in range(wide)
+            ],
+            axis=1,
+        ),
+        count,
+    )
+    vector_grads = (
+        query_bias_grad,
+        value_bias_grad,
+        out_bias_grad,
+        attn_gain_grad,
+        attn_shift_grad,
+        up_bias_grad,
+        down_bias_grad,
+        ffn_gain_grad,
+        ffn_shift_grad,
+    )
+    flat_grads = jnp.concatenate([v.reshape(count, -1) for v in vector_grads], axis=1)
+    flat_grads = jnp.pad(flat_grads, ((0, 0), (0, spare * D - flat_grads.shape[1])))
+    sum_first = scatter_sum(
+        jnp.concatenate(
+            [g.astype(low).reshape(count, rows, D) for g in (query_grad, key_grad, value_grad)]
+            + [flat_grads.astype(low).reshape(count, spare, D)],
+            axis=1,
+        ),
+        count,
+    )
+    flat_sum = sum_first[3 * rows :].reshape(-1)
+    owned, at = [], 0
+    for size in sizes:
+        owned.append(flat_sum[at : at + size])
+        at += size
+    sum_up = jnp.concatenate(
+        [sum_second[rows * (1 + i) : rows * (2 + i)] for i in range(wide)], axis=1
+    )
+    return (
+        layer_out,
+        input_grad,
+        sum_first[:rows],
+        owned[0],
+        sum_first[rows : 2 * rows],
+        sum_first[2 * rows : 3 * rows],
+        owned[1],
+        sum_second[:rows],
+        owned[2],
+        owned[3],
+        owned[4],
         sum_up,
-        sum_up_bias,
+        owned[5],
         sum_down,
-        sum_down_bias,
-        sum_ffn_gain,
-        sum_ffn_shift,
-    ) = summed_local
-    owned_all = (
-        lax.psum(sum_query.astype(jnp.bfloat16), "rep").astype(jnp.float32),
-        lax.psum(sum_query_bias.astype(jnp.bfloat16), "rep").astype(jnp.float32),
-        lax.psum(sum_key.astype(jnp.bfloat16), "rep").astype(jnp.float32),
-        lax.psum(sum_value.astype(jnp.bfloat16), "rep").astype(jnp.float32),
-        lax.psum(sum_value_bias.astype(jnp.bfloat16), "rep").astype(jnp.float32),
-        lax.psum(sum_out.astype(jnp.bfloat16), "rep").astype(jnp.float32),
-        lax.psum(sum_out_bias.astype(jnp.bfloat16), "rep").astype(jnp.float32),
-        lax.psum(sum_attn_gain.astype(jnp.bfloat16), "rep").astype(jnp.float32),
-        lax.psum(sum_attn_shift.astype(jnp.bfloat16), "rep").astype(jnp.float32),
-        lax.psum(sum_up.astype(jnp.bfloat16), "rep").astype(jnp.float32),
-        lax.psum(sum_up_bias.astype(jnp.bfloat16), "rep").astype(jnp.float32),
-        lax.psum(sum_down.astype(jnp.bfloat16), "rep").astype(jnp.float32),
-        lax.psum(sum_down_bias.astype(jnp.bfloat16), "rep").astype(jnp.float32),
-        lax.psum(sum_ffn_gain.astype(jnp.bfloat16), "rep").astype(jnp.float32),
-        lax.psum(sum_ffn_shift.astype(jnp.bfloat16), "rep").astype(jnp.float32),
-    )
-    return (layer_out, input_grad, *owned_all)
+        owned[6],
+        owned[7],
+        owned[8],
+    )
 
 
 def solution(mesh):

time: 1010 us -> 622 us (0.62)
  waiting for transfers between devices: 447 us -> 180 us
  blocking collectives: 129 us -> 0 us
  matrix products: 288 us -> 244 us
  starting transfers between devices: 0.52 us -> 31.3 us
  other arithmetic: 32.7 us -> 53.2 us
  local copies, waits for them, and re-layouts: 84.9 us -> 103 us
  between operations: 17.9 us -> 2 us
    reduce_scatter x3 -> x0, waiting for transfers between devices: 227 us -> none  [the longest x1 114 us: shards(): lax.psum_scatter(down_grad, 'fsdp', scatter_dimension=0, tiled=True)]
    ppermute x0 -> x27, waiting for transfers between devices: none -> 180 us  [the longest x24 173 us: swap(): return lax.ppermute(value, 'fsdp', [(i, i ^ mask) for i in range(count)])]
    unnamed x16 -> x0, waiting for transfers between devices: 140 us -> none
    unnamed x2 -> x0, blocking collectives: 124 us -> none
    all_gather x6 -> x0, waiting for transfers between devices: 79.9 us -> none  [the longest x1 48.5 us: shards(): lax.all_gather(up_weight, 'fsdp', axis=0, tiled=True)]
    ppermute x0 -> x27, starting transfers between devices: none -> 31.3 us  [the longest x24 26.4 us: swap(): return lax.ppermute(value, 'fsdp', [(i, i ^ mask) for i in range(count)])]
    dot_general x6, matrix products: 74.4 us -> 53.8 us  [project(): return jnp.dot(left, right, preferred_element_type=jnp.float32)]
    another operation x3 -> x24, other arithmetic: 0.01 us -> 20 us  [the longest x21 20 us: gather_rows(): jnp.stack([jnp.where(mine_low, held, other), jnp.where(mine_low, other, h...]
  transfers between devices with their start and end apart: 13 -> 27, of which waited for: 9 -> 14; matrix products, arithmetic and copies ran while one was open for 34% -> 22% of each run, Pallas kernels for 0% -> 0%
where the time goes in v1:
time: 622 us; the launch traced here: 617 us
  matrix products  244 us (39%)
  waiting for transfers between devices  180 us (29%)
  local copies, waits for them, and re-layouts  103 us (17%)
  other arithmetic  53.2 us (9%)
  starting transfers between devices  31.3 us (5%)
    ppermute x24, waiting for transfers between devices, swap(): return lax.ppermute(value, 'fsdp', [(i, i ^ mask) for i in range(count)])  173 us
    dot_general x6, matrix products, project(): return jnp.dot(left, right, preferred_element_type=jnp.float32)  53.8 us
    dot_general x2, matrix products, attend_back(): jnp.einsum('hqk,qhd->khd', grad_raw, query, preferred_element_type=jnp.fl...  41.3 us
    dot_general x2, matrix products, attend_back(): jnp.einsum('hqk,khd->qhd', grad_raw, keys, preferred_element_type=jnp.flo...  40.4 us
    unnamed x148, local copies, waits for them, and re-layouts  34.5 us
    dot_general x6, matrix products, project_back(): jnp.einsum('tb,ab->ta', grad, weight, preferred_element_type=jnp.float32)  28.4 us
    ppermute x24, starting transfers between devices, swap(): return lax.ppermute(value, 'fsdp', [(i, i ^ mask) for i in range(count)])  26.4 us
    dot_general x6, matrix products, contract_rows(): jnp.einsum('ta,tb->ab', left, right, preferred_element_type=jnp.float32)  21.4 us
  transfers between devices with their start and end apart: 27, of which 14 were waited for; matrix products, arithmetic and copies ran while one was open for 22% of the time, Pallas kernels for 0%

profile of v1, /device:TPU:0, one launch (start us, length us, event | category | flops | bytes accessed | tf_op | source)
XLA Modules:
  0.0 617.5 jit_solution(16276279991324245360)
XLA Ops:
  0.7 4.1 collective-permute-start.8
  4.8 6.1 concatenate.45
  16.4 2.9 collective-permute-start.4
  19.3 17.8 %collective-permute-done = bf16[1,145,768]{2,1,0:T(8,128)(2,1)S(1)} collective-permute-done((bf16[1,145,768]{2,1,0:T(8,128)(2,1)S(1)}, bf16[1,145,768]{2,1,0:T(8,128)(2,1)S(1)}, u32[]{:S(2)}, u32[]{:S(2)}) %collective-permute-start) | collective-permute-done | bytes 222752 | tf_op jit(solution)/shard_map/ppermute | solution.py:284
  41.2 3.1 collective-permute-done.4
  45.9 8.3 %collective-permute-done.1 = bf16[2,145,768]{2,1,0:T(8,128)(2,1)S(1)} collective-permute-done((bf16[2,145,768]{2,1,0:T(8,128)(2,1)S(1)}, bf16[2,145,768]{2,1,0:T(8,128)(2,1)S(1)}, u32[]{:S(2)}, u32[]{:S(2)}) %collective-permute-start.1) | collective-permute-done | bytes 445472 | tf_op jit(solution)/shard_map/ppermute | solution.py:284
  57.2 9.8 %collective-permute-done.9 = bf16[2,192,768]{2,1,0:T(8,128)(2,1)} collective-permute-done((bf16[2,192,768]{2,1,0:T(8,128)(2,1)}, bf16[2,192,768]{2,1,0:T(8,128)(2,1)}, u32[]{:S(2)}, u32[]{:S(2)}) %collective-permute-start.9) | collective-permute-done | bytes 589856 | tf_op jit(solution)/shard_map/ppermute | solution.py:284
  70.8 11.9 %collective-permute-done.5 = bf16[2,240,768]{2,1,0:T(8,128)(2,1)} collective-permute-done((bf16[2,240,768]{2,1,0:T(8,128)(2,1)}, bf16[2,240,768]{2,1,0:T(8,128)(2,1)}, u32[]{:S(2)}, u32[]{:S(2)}) %collective-permute-start.5) | collective-permute-done | bytes 737312 | tf_op jit(solution)/shard_map/ppermute | solution.py:284
  94.3 9.6 %collective-permute-done.10 = bf16[4,192,768]{2,1,0:T(8,128)(2,1)} collective-permute-done((bf16[4,192,768]{2,1,0:T(8,128)(2,1)}, bf16[4,192,768]{2,1,0:T(8,128)(2,1)}, u32[]{:S(2)}, u32[]{:S(2)}) %collective-permute-start.10) | collective-permute-done | bytes 1179680 | tf_op jit(solution)/shard_map/ppermute | solution.py:284
  107.5 27.0 %collective-permute-done.6 = bf16[4,240,768]{2,1,0:T(8,128)(2,1)} collective-permute-done((bf16[4,240,768]{2,1,0:T(8,128)(2,1)}, bf16[4,240,768]{2,1,0:T(8,128)(2,1)}, u32[]{:S(2)}, u32[]{:S(2)}) %collective-permute-start.6) | collective-permute-done | bytes 1474592 | tf_op jit(solution)/shard_map/ppermute | solution.py:284
  146.8 2.9 reshape.527
  162.5 23.8 %while.30 = (s32[]{:T(128)}, bf16[2,512,12,64]{1,3,2,0:T(8,128)(2,1)}, f32[2,12,512,1]{2,1,3,0:T(8,128)S(1)}, bf16[2,512,12,64]{1,3,2,0:T(8,128)(2,1)}, s32[2]{0...) while((s32[]{:T(128)}, ...), condition=%wide.region_3.4_spmd, body=%wide.region_0.3_spmd.sunk | while | flops 843708928 | bytes 42170484 | solution.py:117
  169.1 5.5 fusion.207
  180.8 5.5 fusion.207
  186.3 4.2 copy.203
  196.2 3.1 select_bitcast_fusion.1
  205.5 37.6 %fusion.98 = (bf16[1024,3072]{1,0:T(8,128)(2,1)}, f32[1024,3072]{1,0:T(8,128)}) fusion(f32[3072]{0:T(1024)S(1)} %reshape.566, bf16[768,768]{1,0:T(8,128)(2,1)S(1)} %bitcast.411, bf16[768,768]{1,0:T(8,128)(2,1)S(1)} %bitcast.413, bf16[768,768]{1,0:T(8,128)(2,1)S(1)} %bitcast.415, bf16[768,768]{1,0:T(8,128)(2,1)S(1)} %bitcast.417, ...), kind=kOutput, calls=%fused_computation.96 | convolution fusion | flops 5062262784 | bytes 26765312 | tf_op jit(solution)/shard_map/dot_general | solution.py:18
  243.1 7.7 %fusion.151 = (f32[1024]{0:T(1024)S(1)}, f32[1024,768]{0,1:T(8,128)S(1)}) fusion(f32[768]{0:T(1024)S(1)} %reshape.567, bf16[1024,3072]{1,0:T(8,128)(2,1)} %get-tuple-element.521, bf16[3072,768]{1,0:T(8,128)(2,1)S(1)} %bitcast.395, f32[768]{0:T(1024)S(1)} %reshape.565, f32[768]{0:T(1024)S(1)} %reshape.564, f32[1024]{0:T(1024)S(1)} %add_rsqrt_fusion.1, ...), kind=kOutput, calls=%fused_computation.287 | convolution fusion | flops 4837342208 | bytes 17323008 | tf_op jit(solution)/shard_map/dot_general | solution.py:18
  252.2 3.2 fusion.121
  257.3 7.0 %convolution_convert_fusion = bf16[3072,768]{1,0:T(8,128)(2,1)} fusion(bf16[1024,3072]{1,0:T(8,128)(2,1)S(1)} %bitcast.433, bf16[1024,768]{0,1:T(8,128)(2,1)S(1)} %get-tuple-element.453), kind=kOutput, calls=%fused_computation.121 | convolution fusion | flops 4834197504 | bytes 12582912 | tf_op jit(solution)/shard_map/ta,tb->ab/dot_general | solution.py:22
  264.3 12.3 %fusion.152 = (bf16[3072]{0:T(1024)(128)(2,1)}, bf16[1024,3072]{1,0:T(8,128)(2,1)S(1)}) fusion(f32[1024,3072]{1,0:T(8,128)} %get-tuple-element.522, f32[3072]{0:T(1024)S(1)} %reshape.566, bf16[1024,768]{0,1:T(8,128)(2,1)S(1)} %get-tuple-element.453, bf16[3072,768]{1,0:T(8,128)(2,1)S(1)} %bitcast.396), kind=kOutput, calls=%fused_computation.288 | convolution fusion | flops 4869583872 | bytes 25184256 | tf_op jit(solution)/shard_map/tb,ab->ta/dot_general | solution.py:26
  279.2 7.2 %convolution_convert_fusion.1 = bf16[768,3072]{1,0:T(8,128)(2,1)} fusion(bf16[1024,3072]{1,0:T(8,128)(2,1)S(1)} %get-tuple-element.527, f32[1024,768]{0,1:T(8,128)S(1)} %get-tuple-element.520, f32[768]{0:T(1024)S(1)} %reshape.565, f32[768]{0:T(1024)S(1)} %reshape.564, f32[1024]{0:T(1024)S(1)} %add_rsqrt_fusion.1, f32[1024]{0:T(1024)S(1)} %broadcast_multiply_fusion.5), kind=kOutput, calls=%fused_computation.122 | convolution fusion | flops 4838129664 | bytes 14170112 | tf_op jit(solution)/shard_map/ta,tb->ab/dot_general | solution.py:22
  286.5 10.2 %multiply_reduce_fusion.1 = (bf16[768]{0:T(1024)(128)(2,1)}, f32[1024]{0:T(1024)S(1)}, f32[1024]{0:T(1024)S(1)}, bf16[768]{0:T(1024)(128)(2,1)}, f32[1024,768]{0,1:T(8,128)S(1)}) fusion(f32[1024,768]{0,1:T(8,128)S(1)} %get-tuple-element.520, f32[1024]{0:T(1024)S(1)} %add_rsqrt_fusion.1, f32[1024]{0:T(1024)S(1)} %broadcast_multiply_fusion.5, ...), kind=kOutput, calls=%fused_computation.139 | convolution fusion | flops 4864864256 | bytes 22062080 | tf_op jit(solution)/shard_map/tb,ab->ta/dot_general | solution.py:26
  304.1 4.0 reshape.545
  308.1 2.9 copy.216
  311.0 128.5 %while.31 = (s32[]{:T(128)}, bf16[2,512,12,64]{1,3,2,0:T(8,128)(2,1)}, bf16[2,512,12,64]{1,3,2,0:T(8,128)(2,1)}, bf16[2,512,12,64]{1,3,2,0:T(8,128)(2,1)}, bf16[...) while((s32[]{:T(128)}, ...), condition=%wide.region_14.15_spmd, body=%wide.region_12.14_spmd.sunk | while | flops 2101626368 | bytes 163005648 | solution.py:242
  311.4 6.4 %fusion.219 = f32[12,512,512]{1,2,0:T(8,128)} fusion(bf16[2,512,12,64]{1,3,2,0:T(8,128)(2,1)S(1)} %get-tuple-element.695, s32[]{:T(128)} %get-tuple-element.677, bf16[2,512,12,64]{1,3,2,0:T(8,128)(2,1)S(1)} %get-tuple-element.693), kind=kOutput, calls=%fused_computation.58.clone.1 | convolution fusion | flops 402653184 | bytes 14156800 | tf_op jit(solution)/shard_map/while/body/eval_jaxpr/qhd,khd->hqk/dot_general | solution.py:61
  317.8 6.4 %fusion.218 = f32[12,512,512]{1,2,0:T(8,128)} fusion(bf16[2,512,12,64]{1,3,2,0:T(8,128)(2,1)S(1)} %copy-done.4, s32[]{:T(128)} %get-tuple-element.677, bf16[2,512,12,64]{1,3,2,0:T(8,128)(2,1)S(1)} %copy-done.5), kind=kOutput, calls=%fused_computation.53.clone.1 | convolution fusion | flops 402653184 | bytes 14156800 | tf_op jit(solution)/shard_map/while/body/eval_jaxpr/qhd,khd->hqk/dot_general | solution.py:81
  325.7 20.6 %bitcast_dynamic-update-slice_fusion.10 = bf16[2,512,12,64]{1,3,2,0:T(8,128)(2,1)} fusion(bf16[2,512,12,64]{1,3,2,0:T(8,128)(2,1)} %get-tuple-element.679, s32[]{:T(128)} %get-tuple-element.677, f32[12,512,512]{1,2,0:T(8,128)} %fusion.218, f32[12,512,512]{1,2,0:T(8,128)} %fusion.219, f32[12,512]{1,0:T(8,128)S(1)} %dynamic-slice_bitcast_fusion.11, ...), kind=kOutput, calls=%fused_computation.51.clone.1 | convolution fusion | flops 440408576 | bytes 53281792 | tf_op jit(solution)/shard_map/while/body/eval_jaxpr/hqk,qhd->khd/dot_general | solution.py:90
  346.3 20.2 %bitcast_dynamic-update-slice_fusion.9 = bf16[2,512,12,64]{1,3,2,0:T(8,128)(2,1)} fusion(bf16[2,512,12,64]{1,3,2,0:T(8,128)(2,1)} %get-tuple-element.678, s32[]{:T(128)} %get-tuple-element.677, f32[12,512,512]{1,2,0:T(8,128)} %fusion.218, f32[12,512,512]{1,2,0:T(8,128)} %fusion.219, f32[12,512]{1,0:T(8,128)S(1)} %dynamic-slice_bitcast_fusion.11, ...), kind=kOutput, calls=%fused_computation.52.clone.1 | convolution fusion | flops 440408576 | bytes 53281792 | tf_op jit(solution)/shard_map/while/body/eval_jaxpr/hqk,khd->qhd/dot_general | solution.py:89
  366.5 8.8 %bitcast_dynamic-update-slice_fusion.11 = bf16[2,512,12,64]{1,3,2,0:T(8,128)(2,1)} fusion(bf16[2,512,12,64]{1,3,2,0:T(8,128)(2,1)} %get-tuple-element.680, s32[]{:T(128)} %get-tuple-element.677, f32[12,512,512]{1,2,0:T(8,128)} %fusion.219, f32[12,512]{1,0:T(8,128)S(1)} %dynamic-slice_bitcast_fusion.11, ...), kind=kOutput, calls=%fused_computation.50.clone.1 | convolution fusion | flops 415236096 | bytes 15229952 | tf_op jit(solution)/shard_map/while/body/eval_jaxpr/hqk,qhd->khd/dot_general | solution.py:84
  375.3 6.4 %fusion.219 = f32[12,512,512]{1,2,0:T(8,128)} fusion(bf16[2,512,12,64]{1,3,2,0:T(8,128)(2,1)S(1)} %get-tuple-element.695, s32[]{:T(128)} %get-tuple-element.677, bf16[2,512,12,64]{1,3,2,0:T(8,128)(2,1)S(1)} %get-tuple-element.693), kind=kOutput, calls=%fused_computation.58.clone.1 | convolution fusion | flops 402653184 | bytes 14156800 | tf_op jit(solution)/shard_map/while/body/eval_jaxpr/qhd,khd->hqk/dot_general | solution.py:61
  381.8 6.4 %fusion.218 = f32[12,512,512]{1,2,0:T(8,128)} fusion(bf16[2,512,12,64]{1,3,2,0:T(8,128)(2,1)S(1)} %copy-done.4, s32[]{:T(128)} %get-tuple-element.677, bf16[2,512,12,64]{1,3,2,0:T(8,128)(2,1)S(1)} %copy-done.5), kind=kOutput, calls=%fused_computation.53.clone.1 | convolution fusion | flops 402653184 | bytes 14156800 | tf_op jit(solution)/shard_map/while/body/eval_jaxpr/qhd,khd->hqk/dot_general | solution.py:81
  389.6 20.7 %bitcast_dynamic-update-slice_fusion.10 = bf16[2,512,12,64]{1,3,2,0:T(8,128)(2,1)} fusion(bf16[2,512,12,64]{1,3,2,0:T(8,128)(2,1)} %get-tuple-element.679, s32[]{:T(128)} %get-tuple-element.677, f32[12,512,512]{1,2,0:T(8,128)} %fusion.218, f32[12,512,512]{1,2,0:T(8,128)} %fusion.219, f32[12,512]{1,0:T(8,128)S(1)} %dynamic-slice_bitcast_fusion.11, ...), kind=kOutput, calls=%fused_computation.51.clone.1 | convolution fusion | flops 440408576 | bytes 53281792 | tf_op jit(solution)/shard_map/while/body/eval_jaxpr/hqk,qhd->khd/dot_general | solution.py:90
  410.3 20.2 %bitcast_dynamic-update-slice_fusion.9 = bf16[2,512,12,64]{1,3,2,0:T(8,128)(2,1)} fusion(bf16[2,512,12,64]{1,3,2,0:T(8,128)(2,1)} %get-tuple-element.678, s32[]{:T(128)} %get-tuple-element.677, f32[12,512,512]{1,2,0:T(8,128)} %fusion.218, f32[12,512,512]{1,2,0:T(8,128)} %fusion.219, f32[12,512]{1,0:T(8,128)S(1)} %dynamic-slice_bitcast_fusion.11, ...), kind=kOutput, calls=%fused_computation.52.clone.1 | convolution fusion | flops 440408576 | bytes 53281792 | tf_op jit(solution)/shard_map/while/body/eval_jaxpr/hqk,khd->qhd/dot_general | solution.py:89
  430.5 8.8 %bitcast_dynamic-update-slice_fusion.11 = bf16[2,512,12,64]{1,3,2,0:T(8,128)(2,1)} fusion(bf16[2,512,12,64]{1,3,2,0:T(8,128)(2,1)} %get-tuple-element.680, s32[]{:T(128)} %get-tuple-element.677, f32[12,512,512]{1,2,0:T(8,128)} %fusion.219, f32[12,512]{1,0:T(8,128)S(1)} %dynamic-slice_bitcast_fusion.11, ...), kind=kOutput, calls=%fused_computation.50.clone.1 | convolution fusion | flops 415236096 | bytes 15229952 | tf_op jit(solution)/shard_map/while/body/eval_jaxpr/hqk,qhd->khd/dot_general | solution.py:84
  441.3 4.2 copy.218
  447.4 3.2 dynamic-slice_bitcast_fusion.2
  451.2 4.6 fusion.146
  482.7 3.1 fusion.113
  486.4 17.3 %collective-permute-done.13 = bf16[4,145,768]{2,0,1:T(4,128)(2,1)S(1)} collective-permute-done((bf16[4,145,768]{2,0,1:T(4,128)(2,1)S(1)}, bf16[4,145,768]{2,0,1:T(4,128)(2,1)S(1)}, u32[]{:S(2)}, u32[]{:S(2)}) %collective-permute-start.13) | collective-permute-done | bytes 890912 | tf_op jit(solution)/shard_map/ppermute | solution.py:284
  509.9 5.8 collective-permute-done.14
  519.7 8.0 %collective-permute-done.15 = bf16[1,145,768]{2,1,0:T(8,128)(2,1)S(1)} collective-permute-done((bf16[1,145,768]{2,1,0:T(8,128)(2,1)S(1)}, bf16[1,145,768]{2,1,0:T(8,128)(2,1)S(1)}, u32[]{:S(2)}, u32[]{:S(2)}) %collective-permute-start.15) | collective-permute-done | bytes 222752 | tf_op jit(solution)/shard_map/ppermute | solution.py:284
  531.4 28.7 %collective-permute-done.18 = bf16[4,240,768]{2,1,0:T(8,128)(2,1)S(1)} collective-permute-done((bf16[4,240,768]{2,1,0:T(8,128)(2,1)S(1)}, bf16[4,240,768]{2,1,0:T(8,128)(2,1)S(1)}, u32[]{:S(2)}, u32[]{:S(2)}) %collective-permute-start.18) | collective-permute-done | bytes 1474592 | tf_op jit(solution)/shard_map/ppermute | solution.py:284
  571.5 4.2 collective-permute-start.25
  575.7 10.8 %collective-permute-done.19 = bf16[2,240,768]{2,1,0:T(8,128)(2,1)} collective-permute-done((bf16[2,240,768]{2,1,0:T(8,128)(2,1)}, bf16[2,240,768]{2,1,0:T(8,128)(2,1)}, u32[]{:S(2)}, u32[]{:S(2)}) %collective-permute-start.19) | collective-permute-done | bytes 737312 | tf_op jit(solution)/shard_map/ppermute | solution.py:284
  590.4 14.5 %collective-permute-done.20 = bf16[1,240,768]{2,1,0:T(8,128)(2,1)S(1)} collective-permute-done((bf16[1,240,768]{2,1,0:T(8,128)(2,1)S(1)}, bf16[1,240,768]{2,1,0:T(8,128)(2,1)S(1)}, u32[]{:S(2)}, u32[]{:S(2)}) %collective-permute-start.20) | collective-permute-done | bytes 368672 | tf_op jit(solution)/shard_map/ppermute | solution.py:284
  608.1 7.4 %collective-permute-done.21 = bf16[240,768]{1,0:T(8,128)(2,1)S(1)} collective-permute-done((bf16[240,768]{1,0:T(8,128)(2,1)S(1)}, bf16[240,768]{1,0:T(8,128)(2,1)S(1)}, u32[]{:S(2)}, u32[]{:S(2)}) %collective-permute-start.21) | collective-permute-done | bytes 368672 | tf_op jit(solution)/shard_map/ppermute | solution.py:315
  (350 shorter events, 161.2 us)
Async XLA Ops:
  0.7 37.6 %copy-start.49 = (bf16[192,768]{1,0:T(8,128)(2,1)S(1)}, bf16[192,768]{1,0:T(8,128)(2,1)}, u32[]{:S(2)}) copy-start(bf16[192,768]{1,0:T(8,128)(2,1)} %param.35) | copy-start | bytes 884740
  0.7 37.6 %collective-permute-start.8 = (bf16[1,192,768]{2,1,0:T(8,128)(2,1)}, bf16[1,192,768]{2,1,0:T(8,128)(2,1)S(1)}, u32[]{:S(2)}, u32[]{:S(2)}) collective-permute-start(bf16[1,192,768]{2,1,0:T(8,128)(2,1)} %bitcast.428), channel_id=1, source_target_pairs={{0,8},{1,9},{2,10},{3,11},{4,12},{5,13},{6,14},{7,15},{8,0},{9,1},... | collective-permute-start | bytes 884744 | tf_op jit(solution)/shard_map/ppermute | solution.py:284
  11.9 25.2 %collective-permute-start = (bf16[1,145,768]{2,1,0:T(8,128)(2,1)S(1)}, bf16[1,145,768]{2,1,0:T(8,128)(2,1)S(1)}, u32[]{:S(2)}, u32[]{:S(2)}) collective-permute-start(bf16[1,145,768]{2,1,0:T(8,128)(2,1)S(1)} %maximum_bitcast_fusion.3), channel_id=1, source_target_pairs={{0,8},{1,9},{2,10},{3,11},{4,12},{5,13},{6,14},{7,15},{8,0},{9,1},... | collective-permute-start | bytes 668168 | tf_op jit(solution)/shard_map/ppermute | solution.py:284
  16.4 27.8 %collective-permute-start.4 = (bf16[1,240,768]{2,1,0:T(8,128)(2,1)S(1)}, bf16[1,240,768]{2,1,0:T(8,128)(2,1)S(1)}, u32[]{:S(2)}, u32[]{:S(2)}) collective-permute-start(bf16[1,240,768]{2,1,0:T(8,128)(2,1)S(1)} %bitcast.427), channel_id=1, source_target_pairs={{0,8},{1,9},{2,10},{3,11},{4,12},{5,13},{6,14},{7,15},{8,0},{9,1},... | collective-permute-start | bytes 1105928 | tf_op jit(solution)/shard_map/ppermute | solution.py:284
  38.1 16.1 %collective-permute-start.1 = (bf16[2,145,768]{2,1,0:T(8,128)(2,1)S(1)}, bf16[2,145,768]{2,1,0:T(8,128)(2,1)S(1)}, u32[]{:S(2)}, u32[]{:S(2)}) collective-permute-start(bf16[2,145,768]{2,1,0:T(8,128)(2,1)S(1)} %maximum_bitcast_fusion.2), channel_id=1, source_target_pairs={{0,4},{1,5},{2,6},{3,7},{4,0},{5,1},{6,2},{7,3},{8,12},{9,13},{10,... | collective-permute-start | bytes 1336328 | tf_op jit(solution)/shard_map/ppermute | solution.py:284
  39.2 27.8 %collective-permute-start.9 = (bf16[2,192,768]{2,1,0:T(8,128)(2,1)}, bf16[2,192,768]{2,1,0:T(8,128)(2,1)}, u32[]{:S(2)}, u32[]{:S(2)}) collective-permute-start(bf16[2,192,768]{2,1,0:T(8,128)(2,1)} %maximum_bitcast_fusion.1), channel_id=1, source_target_pairs={{0,4},{1,5},{2,6},{3,7},{4,0},{5,1},{6,2},{7,3},{8,12},{9,13},{10,... | collective-permute-start | bytes 1769480 | tf_op jit(solution)/shard_map/ppermute | solution.py:284
  45.2 37.5 %collective-permute-start.5 = (bf16[2,240,768]{2,1,0:T(8,128)(2,1)}, bf16[2,240,768]{2,1,0:T(8,128)(2,1)}, u32[]{:S(2)}, u32[]{:S(2)}) collective-permute-start(bf16[2,240,768]{2,1,0:T(8,128)(2,1)} %maximum_bitcast_fusion), channel_id=1, source_target_pairs={{0,4},{1,5},{2,6},{3,7},{4,0},{5,1},{6,2},{7,3},{8,12},{9,13},{10,... | collective-permute-start | bytes 2211848 | tf_op jit(solution)/shard_map/ppermute | solution.py:284
  55.6 31.0 %collective-permute-start.2 = (bf16[4,145,768]{2,0,1:T(4,128)(2,1)}, bf16[4,145,768]{2,0,1:T(4,128)(2,1)S(1)}, u32[]{:S(2)}, u32[]{:S(2)}) collective-permute-start(bf16[4,145,768]{2,0,1:T(4,128)(2,1)} %copy.192), channel_id=1, source_target_pairs={{0,2},{1,3},{2,0},{3,1},{4,6},{5,7},{6,4},{7,5},{8,10},{9,11},{10,... | collective-permute-start | bytes 2672648 | tf_op jit(solution)/shard_map/ppermute | solution.py:284
  69.3 34.6 %collective-permute-start.10 = (bf16[4,192,768]{2,1,0:T(8,128)(2,1)}, bf16[4,192,768]{2,1,0:T(8,128)(2,1)}, u32[]{:S(2)}, u32[]{:S(2)}) collective-permute-start(bf16[4,192,768]{2,1,0:T(8,128)(2,1)} %bitcast.65), channel_id=1, source_target_pairs={{0,2},{1,3},{2,0},{3,1},{4,6},{5,7},{6,4},{7,5},{8,10},{9,11},{10,... | collective-permute-start | bytes 3538952 | tf_op jit(solution)/shard_map/ppermute | solution.py:284
  85.1 49.3 %collective-permute-start.6 = (bf16[4,240,768]{2,1,0:T(8,128)(2,1)}, bf16[4,240,768]{2,1,0:T(8,128)(2,1)}, u32[]{:S(2)}, u32[]{:S(2)}) collective-permute-start(bf16[4,240,768]{2,1,0:T(8,128)(2,1)} %bitcast.46), channel_id=1, source_target_pairs={{0,2},{1,3},{2,0},{3,1},{4,6},{5,7},{6,4},{7,5},{8,10},{9,11},{10,... | collective-permute-start | bytes 4423688 | tf_op jit(solution)/shard_map/ppermute | solution.py:284
  88.8 49.7 %collective-permute-start.3 = (bf16[8,145,768]{2,0,1:T(8,128)(2,1)}, bf16[8,145,768]{2,0,1:T(8,128)(2,1)}, u32[]{:S(2)}, u32[]{:S(2)}) collective-permute-start(bf16[8,145,768]{2,0,1:T(8,128)(2,1)} %copy.196), channel_id=1, source_target_pairs={{0,1},{1,0},{2,3},{3,2},{4,5},{5,4},{6,7},{7,6},{8,9},{9,8},{10,11... | collective-permute-start | bytes 5345288 | tf_op jit(solution)/shard_map/ppermute | solution.py:284
  107.5 85.2 %collective-permute-start.11 = (bf16[8,192,768]{2,1,0:T(8,128)(2,1)}, bf16[8,192,768]{2,1,0:T(8,128)(2,1)}, u32[]{:S(2)}, u32[]{:S(2)}) collective-permute-start(bf16[8,192,768]{2,1,0:T(8,128)(2,1)} %bitcast.68), channel_id=1, source_target_pairs={{0,1},{1,0},{2,3},{3,2},{4,5},{5,4},{6,7},{7,6},{8,9},{9,8},{10,11... | collective-permute-start | bytes 7077896 | tf_op jit(solution)/shard_map/ppermute | solution.py:284
  138.5 57.6 %collective-permute-start.7 = (bf16[8,240,768]{2,1,0:T(8,128)(2,1)}, bf16[8,240,768]{2,1,0:T(8,128)(2,1)}, u32[]{:S(2)}, u32[]{:S(2)}) collective-permute-start(bf16[8,240,768]{2,1,0:T(8,128)(2,1)} %bitcast.49), channel_id=1, source_target_pairs={{0,1},{1,0},{2,3},{3,2},{4,5},{5,4},{6,7},{7,6},{8,9},{9,8},{10,11... | collective-permute-start | bytes 8847368 | tf_op jit(solution)/shard_map/ppermute | solution.py:284
  279.2 7.2 %copy-start.42 = (bf16[16,48,768]{2,1,0:T(8,128)(2,1)S(1)}, bf16[16,48,768]{2,1,0:T(8,128)(2,1)}, u32[]{:S(2)}) copy-start(bf16[16,48,768]{2,1,0:T(8,128)(2,1)} %get-tuple-element.462) | copy-start | bytes 3538948
  304.1 6.9 %copy-start.1 = (bf16[2,512,12,64]{1,3,2,0:T(8,128)(2,1)S(1)}, bf16[2,512,12,64]{1,3,2,0:T(8,128)(2,1)}, u32[]{:S(2)}) copy-start(bf16[2,512,12,64]{1,3,2,0:T(8,128)(2,1)} %copy-done) | copy-start | bytes 4718596
  304.1 6.9 %copy-start.3 = (bf16[2,512,12,64]{1,3,2,0:T(8,128)(2,1)S(1)}, bf16[2,512,12,64]{1,3,2,0:T(8,128)(2,1)}, u32[]{:S(2)}) copy-start(bf16[2,512,12,64]{1,3,2,0:T(8,128)(2,1)} %copy-done.2) | copy-start | bytes 4718596
  304.1 6.9 %copy-start.48 = (f32[2,12,512,1]{2,1,3,0:T(8,128)S(1)}, f32[2,12,512,1]{2,1,3,0:T(8,128)}, u32[]{:S(2)}) copy-start(f32[2,12,512,1]{2,1,3,0:T(8,128)} %copy-done.47) | copy-start | bytes 147460
  304.1 6.9 %copy-start.58 = (s32[2]{0:T(128)S(1)}, s32[2]{0:T(128)}, u32[]{:S(2)}) copy-start(s32[2]{0:T(128)} %param.23) | copy-start | bytes 28
  450.6 6.6 %copy-start.56 = (bf16[768]{0:T(1024)(128)(2,1)S(1)}, bf16[768]{0:T(1024)(128)(2,1)}, u32[]{:S(2)}) copy-start(bf16[768]{0:T(1024)(128)(2,1)} %get-tuple-element.411) | copy-start | bytes 4612
  450.6 6.7 %copy-start.55 = (bf16[768]{0:T(1024)(128)(2,1)S(1)}, bf16[768]{0:T(1024)(128)(2,1)}, u32[]{:S(2)}) copy-start(bf16[768]{0:T(1024)(128)(2,1)} %get-tuple-element.416) | copy-start | bytes 4612
  450.6 6.8 %copy-start.54 = (bf16[3072]{0:T(1024)(128)(2,1)S(1)}, bf16[3072]{0:T(1024)(128)(2,1)}, u32[]{:S(2)}) copy-start(bf16[3072]{0:T(1024)(128)(2,1)} %get-tuple-element.526) | copy-start | bytes 18436
  450.6 6.9 %copy-start.51 = (bf16[768]{0:T(1024)(128)(2,1)S(1)}, bf16[768]{0:T(1024)(128)(2,1)}, u32[]{:S(2)}) copy-start(bf16[768]{0:T(1024)(128)(2,1)} %get-tuple-element.452) | copy-start | bytes 4612
  450.6 7.0 %copy-start.52 = (bf16[768]{0:T(1024)(128)(2,1)S(1)}, bf16[768]{0:T(1024)(128)(2,1)}, u32[]{:S(2)}) copy-start(bf16[768]{0:T(1024)(128)(2,1)} %get-tuple-element.413) | copy-start | bytes 4612
  450.6 7.1 %copy-start.50 = (bf16[16,48]{1,0:T(8,128)(2,1)S(1)}, bf16[16,48]{1,0:T(8,128)(2,1)}, u32[]{:S(2)}) copy-start(bf16[16,48]{1,0:T(8,128)(2,1)} %reshape.554) | copy-start | bytes 4612
  450.6 32.0 %collective-permute-start.22 = (bf16[8,192,768]{2,1,0:T(8,128)(2,1)}, bf16[8,192,768]{2,1,0:T(8,128)(2,1)}, u32[]{:S(2)}, u32[]{:S(2)}) collective-permute-start(bf16[8,192,768]{2,1,0:T(8,128)(2,1)} %dynamic-slice_bitcast_fusion.2), channel_id=1, source_target_pairs={{0,1},{1,0},{2,3},{3,2},{4,5},{5,4},{6,7},{7,6},{8,9},{9,8},{10,11... | collective-permute-start | bytes 7077896 | tf_op jit(solution)/shard_map/ppermute | solution.py:284
  469.9 7.1 %collective-permute-start.12 = (bf16[8,145,768]{2,0,1:T(8,128)(2,1)}, bf16[8,145,768]{2,0,1:T(8,128)(2,1)S(1)}, u32[]{:S(2)}, u32[]{:S(2)}) collective-permute-start(bf16[8,145,768]{2,0,1:T(8,128)(2,1)} %dynamic-slice_bitcast_fusion.3), channel_id=1, source_target_pairs={{0,1},{1,0},{2,3},{3,2},{4,5},{5,4},{6,7},{7,6},{8,9},{9,8},{10,11... | collective-permute-start | bytes 5345288 | tf_op jit(solution)/shard_map/ppermute | solution.py:284
  476.9 27.1 %collective-permute-start.17 = (bf16[8,240,768]{2,1,0:T(8,128)(2,1)}, bf16[8,240,768]{2,1,0:T(8,128)(2,1)}, u32[]{:S(2)}, u32[]{:S(2)}) collective-permute-start(bf16[8,240,768]{2,1,0:T(8,128)(2,1)} %dynamic-slice_bitcast_fusion.1), channel_id=1, source_target_pairs={{0,1},{1,0},{2,3},{3,2},{4,5},{5,4},{6,7},{7,6},{8,9},{9,8},{10,11... | collective-permute-start | bytes 8847368 | tf_op jit(solution)/shard_map/ppermute | solution.py:284
  481.0 22.7 %collective-permute-start.13 = (bf16[4,145,768]{2,0,1:T(4,128)(2,1)S(1)}, bf16[4,145,768]{2,0,1:T(4,128)(2,1)S(1)}, u32[]{:S(2)}, u32[]{:S(2)}) collective-permute-start(bf16[4,145,768]{2,0,1:T(4,128)(2,1)S(1)} %copy.229), channel_id=1, source_target_pairs={{0,2},{1,3},{2,0},{3,1},{4,6},{5,7},{6,4},{7,5},{8,10},{9,11},{10,... | collective-permute-start | bytes 2672648 | tf_op jit(solution)/shard_map/ppermute | solution.py:284
  482.6 21.4 %slice-start.2 = ((s8[5898240]{0:T(1024)(128)(4,1)}), s8[1703936]{0:T(1024)(128)(4,1)S(1)}, s32[]{:S(2)}) async-start(s8[5898240]{0:T(1024)(128)(4,1)} %bitcast.376), calls=%async_computation.2 | async-start | bytes 3407872
  482.6 21.0 %copy-start.11 = (bf16[8,145,768]{2,1,0:T(8,128)(2,1)S(1)}, bf16[8,145,768]{2,1,0:T(8,128)(2,1)}, u32[]{:S(2)}) copy-start(bf16[8,145,768]{2,1,0:T(8,128)(2,1)} %copy-done.10) | copy-start | bytes 5345284
  482.6 21.4 %slice-start.3 = ((s8[5898240]{0:T(1024)(128)(4,1)}), s8[4194304]{0:T(1024)(128)(4,1)S(1)}, s32[]{:S(2)}) async-start(s8[5898240]{0:T(1024)(128)(4,1)} %bitcast.376), calls=%async_computation.3 | async-start | bytes 8388608
  485.9 43.6 %collective-permute-start.23 = (bf16[4,192,768]{2,1,0:T(8,128)(2,1)S(1)}, bf16[4,192,768]{2,1,0:T(8,128)(2,1)S(1)}, u32[]{:S(2)}, u32[]{:S(2)}) collective-permute-start(bf16[4,192,768]{2,1,0:T(8,128)(2,1)S(1)} %dynamic-slice_bitcast_fusion.5), channel_id=1, source_target_pairs={{0,2},{1,3},{2,0},{3,1},{4,6},{5,7},{6,4},{7,5},{8,10},{9,11},{10,... | collective-permute-start | bytes 3538952 | tf_op jit(solution)/shard_map/ppermute | solution.py:284
  503.9 11.8 %collective-permute-start.14 = (bf16[2,145,768]{2,1,0:T(8,128)(2,1)S(1)}, bf16[2,145,768]{2,1,0:T(8,128)(2,1)S(1)}, u32[]{:S(2)}, u32[]{:S(2)}) collective-permute-start(bf16[2,145,768]{2,1,0:T(8,128)(2,1)S(1)} %dynamic-slice_bitcast_fusion.9), channel_id=1, source_target_pairs={{0,4},{1,5},{2,6},{3,7},{4,0},{5,1},{6,2},{7,3},{8,12},{9,13},{10,... | collective-permute-start | bytes 1336328 | tf_op jit(solution)/shard_map/ppermute | solution.py:284
  506.9 11.5 %copy-start.34 = (bf16[96,8,2,512]{3,1,2,0:T(8,128)(2,1)S(1)}, bf16[96,8,2,512]{3,1,2,0:T(8,128)(2,1)}, u32[]{:S(2)}) copy-start(bf16[96,8,2,512]{3,1,2,0:T(8,128)(2,1)} %copy-done.33) | copy-start | bytes 4718596
  506.9 11.5 %copy-start.43 = (bf16[16,48,768]{2,1,0:T(8,128)(2,1)S(1)}, bf16[16,48,768]{2,1,0:T(8,128)(2,1)}, u32[]{:S(2)}) copy-start(bf16[16,48,768]{2,1,0:T(8,128)(2,1)} %get-tuple-element.472) | copy-start | bytes 3538948
  506.9 53.2 %collective-permute-start.18 = (bf16[4,240,768]{2,1,0:T(8,128)(2,1)S(1)}, bf16[4,240,768]{2,1,0:T(8,128)(2,1)S(1)}, u32[]{:S(2)}, u32[]{:S(2)}) collective-permute-start(bf16[4,240,768]{2,1,0:T(8,128)(2,1)S(1)} %dynamic-slice_bitcast_fusion.4), channel_id=1, source_target_pairs={{0,2},{1,3},{2,0},{3,1},{4,6},{5,7},{6,4},{7,5},{8,10},{9,11},{10,... | collective-permute-start | bytes 4423688 | tf_op jit(solution)/shard_map/ppermute | solution.py:284
  515.9 11.8 %collective-permute-start.15 = (bf16[1,145,768]{2,1,0:T(8,128)(2,1)S(1)}, bf16[1,145,768]{2,1,0:T(8,128)(2,1)S(1)}, u32[]{:S(2)}, u32[]{:S(2)}) collective-permute-start(bf16[1,145,768]{2,1,0:T(8,128)(2,1)S(1)} %constant_dynamic-slice_fusion.2), channel_id=1, source_target_pairs={{0,8},{1,9},{2,10},{3,11},{4,12},{5,13},{6,14},{7,15},{8,0},{9,1},... | collective-permute-start | bytes 668168 | tf_op jit(solution)/shard_map/ppermute | solution.py:284
  527.8 40.8 %collective-permute-start.16 = (bf16[145,768]{1,0:T(8,128)(2,1)S(1)}, bf16[145,768]{1,0:T(8,128)(2,1)}, u32[]{:S(2)}, u32[]{:S(2)}) collective-permute-start(bf16[145,768]{1,0:T(8,128)(2,1)S(1)} %fusion.136), channel_id=1, source_target_pairs={{0,16},{16,0},{1,17},{17,1},{2,18},{18,2},{3,19},{19,3},{4,20},{20... | collective-permute-start | bytes 668168 | tf_op jit(solution)/shard_map/ppermute | solution.py:315
  530.7 31.3 %copy-start.8 = (f32[1024,768]{0,1:T(8,128)S(1)}, f32[1024,768]{0,1:T(8,128)}, u32[]{:S(2)}) copy-start(f32[1024,768]{0,1:T(8,128)} %copy-done.7) | copy-start | bytes 9437188
  530.7 31.3 %copy-start.16 = (bf16[96,8,2,512]{3,1,2,0:T(8,128)(2,1)S(1)}, bf16[96,8,2,512]{3,1,2,0:T(8,128)(2,1)}, u32[]{:S(2)}) copy-start(bf16[96,8,2,512]{3,1,2,0:T(8,128)(2,1)} %copy-done.15) | copy-start | bytes 4718596
  530.7 31.3 %copy-start.27 = (bf16[16,48,768]{2,1,0:T(8,128)(2,1)S(1)}, bf16[16,48,768]{2,1,0:T(8,128)(2,1)}, u32[]{:S(2)}) copy-start(bf16[16,48,768]{2,1,0:T(8,128)(2,1)} %copy-done.26) | copy-start | bytes 3538948
  530.7 39.6 %collective-permute-start.24 = (bf16[2,192,768]{2,1,0:T(8,128)(2,1)}, bf16[2,192,768]{2,1,0:T(8,128)(2,1)}, u32[]{:S(2)}, u32[]{:S(2)}) collective-permute-start(bf16[2,192,768]{2,1,0:T(8,128)(2,1)} %dynamic-slice_bitcast_fusion.8), channel_id=1, source_target_pairs={{0,4},{1,5},{2,6},{3,7},{4,0},{5,1},{6,2},{7,3},{8,12},{9,13},{10,... | collective-permute-start | bytes 1769480 | tf_op jit(solution)/shard_map/ppermute | solution.py:284
  562.0 24.5 %collective-permute-start.19 = (bf16[2,240,768]{2,1,0:T(8,128)(2,1)}, bf16[2,240,768]{2,1,0:T(8,128)(2,1)}, u32[]{:S(2)}, u32[]{:S(2)}) collective-permute-start(bf16[2,240,768]{2,1,0:T(8,128)(2,1)} %dynamic-slice_bitcast_fusion.7), channel_id=1, source_target_pairs={{0,4},{1,5},{2,6},{3,7},{4,0},{5,1},{6,2},{7,3},{8,12},{9,13},{10,... | collective-permute-start | bytes 2211848 | tf_op jit(solution)/shard_map/ppermute | solution.py:284
  565.9 20.6 %copy-start.19 = (bf16[4,240,768]{2,1,0:T(8,128)(2,1)S(1)}, bf16[4,240,768]{2,1,0:T(8,128)(2,1)}, u32[]{:S(2)}) copy-start(bf16[4,240,768]{2,1,0:T(8,128)(2,1)} %copy-done.18) | copy-start | bytes 4423684
  571.5 17.1 %collective-permute-start.25 = (bf16[1,192,768]{2,1,0:T(8,128)(2,1)S(1)}, bf16[1,192,768]{2,1,0:T(8,128)(2,1)S(1)}, u32[]{:S(2)}, u32[]{:S(2)}) collective-permute-start(bf16[1,192,768]{2,1,0:T(8,128)(2,1)S(1)} %constant_dynamic-slice_fusion), channel_id=1, source_target_pairs={{0,8},{1,9},{2,10},{3,11},{4,12},{5,13},{6,14},{7,15},{8,0},{9,1},... | collective-permute-start | bytes 884744 | tf_op jit(solution)/shard_map/ppermute | solution.py:284
  587.8 17.1 %collective-permute-start.20 = (bf16[1,240,768]{2,1,0:T(8,128)(2,1)S(1)}, bf16[1,240,768]{2,1,0:T(8,128)(2,1)S(1)}, u32[]{:S(2)}, u32[]{:S(2)}) collective-permute-start(bf16[1,240,768]{2,1,0:T(8,128)(2,1)S(1)} %constant_dynamic-slice_fusion.1), channel_id=1, source_target_pairs={{0,8},{1,9},{2,10},{3,11},{4,12},{5,13},{6,14},{7,15},{8,0},{9,1},... | collective-permute-start | bytes 1105928 | tf_op jit(solution)/shard_map/ppermute | solution.py:284
  588.8 18.5 %collective-permute-start.26 = (bf16[192,768]{1,0:T(8,128)(2,1)S(1)}, bf16[192,768]{1,0:T(8,128)(2,1)S(1)}, u32[]{:S(2)}, u32[]{:S(2)}) collective-permute-start(bf16[192,768]{1,0:T(8,128)(2,1)S(1)} %fusion.135), channel_id=1, source_target_pairs={{0,16},{16,0},{1,17},{17,1},{2,18},{18,2},{3,19},{19,3},{4,20},{20... | collective-permute-start | bytes 884744 | tf_op jit(solution)/shard_map/ppermute | solution.py:315
  605.0 10.6 %collective-permute-start.21 = (bf16[240,768]{1,0:T(8,128)(2,1)S(1)}, bf16[240,768]{1,0:T(8,128)(2,1)S(1)}, u32[]{:S(2)}, u32[]{:S(2)}) collective-permute-start(bf16[240,768]{1,0:T(8,128)(2,1)S(1)} %fusion.133), channel_id=1, source_target_pairs={{0,16},{16,0},{1,17},{17,1},{2,18},{18,2},{3,19},{19,3},{4,20},{20... | collective-permute-start | bytes 1105928 | tf_op jit(solution)/shard_map/ppermute | solution.py:315
  (47 other events, 154.6 us)

commit v2 on v1

v2 whole, which is shorter than its diff:
```python
import jax
import jax.numpy as jnp
from jax import lax
from jax.experimental import pallas as pl
from jax.experimental.pallas import tpu as pltpu
from jax.sharding import PartitionSpec as P

D = 768
H = 12
HD = 64
LONG = 512
SHORT = 128
QUAD = 256
PAIR = 128
TILE = 768

EPSILON = 1e-05
BLOCKED = -1e30
LOW = jnp.bfloat16
WIDE = jnp.float32
ROOM = 56 << 20

QUERY_BIAS, VALUE_BIAS, OUT_BIAS, ATTN_GAIN, ATTN_SHIFT, DOWN_BIAS, FFN_GAIN, FFN_SHIFT = range(8)


def dot(left, right, left_dim, right_dim):
    return lax.dot_general(
        left, right, (((left_dim,), (right_dim,)), ((), ())), preferred_element_type=WIDE
    )


def row_mean(value):
    return jnp.mean(value, axis=-1, keepdims=True)


def token_sum(value):
    return jnp.sum(value, axis=0, keepdims=True)


def whole(shape):
    zeros = (0,) * len(shape)
    return pl.BlockSpec(shape, lambda *_: zeros, pipeline_mode=pl.Buffered(1))


def flat(ref):
    value = ref[...]
    return value.reshape(-1, value.shape[-1])


def params():
    return pltpu.CompilerParams(vmem_limit_bytes=ROOM)


def cost(flops, moved, transcendentals=0):
    return pl.CostEstimate(
        flops=int(flops), bytes_accessed=int(moved), transcendentals=int(transcendentals)
    )


def half_masks():
    lane = lax.broadcasted_iota(jnp.int32, (1, PAIR), 1)
    return [jnp.where(lane // HD == half, 1.0, 0.0) for half in range(2)]


def attend_kernel(
    kind_ref,
    x_ref,
    wq_ref,
    wk_ref,
    wv_ref,
    vec_ref,
    q_ref,
    k_ref,
    v_ref,
    ctx_ref,
    ctxt_ref,
    raised_ref,
    inv_ref,
):
    x = x_ref[...]
    q_ref[...] = (dot(x, flat(wq_ref), 1, 0) + vec_ref[QUERY_BIAS : QUERY_BIAS + 1]).astype(LOW)
    k_ref[...] = dot(x, flat(wk_ref), 1, 0).astype(LOW)
    v_ref[...] = (dot(x, flat(wv_ref), 1, 0) + vec_ref[VALUE_BIAS : VALUE_BIAS + 1]).astype(LOW)
    part = lax.broadcasted_iota(jnp.int32, (LONG, PAIR), 0) // SHORT
    lane = lax.broadcasted_iota(jnp.int32, (LONG, PAIR), 1)
    blocked = jnp.where(kind_ref[pl.program_id(1)] == 1, 0.0, BLOCKED)
    query_part = jnp.where((lane < LONG // SHORT) & (part != lane), blocked, 0.0).astype(LOW)
    key_part = jnp.where(part == lane, 1.0, 0.0).astype(LOW)
    halves = half_masks()
    for pair in range(QUAD // PAIR):
        cols = pl.ds(pair * PAIR, PAIR)
        q2 = q_ref[:, cols].astype(WIDE) * HD ** (-0.5)
        keys = jnp.concatenate([k_ref[:, cols], key_part], axis=1)
        v2t = v_ref[:, cols].T
        contexts, inverses = [], []
        for half in range(2):
            queries = jnp.concatenate([(q2 * halves[half]).astype(LOW), query_part], axis=1)
            scores = dot(keys, queries, 1, 1)
            peak = jnp.max(scores, axis=0, keepdims=True)
            raised = jnp.exp(scores - peak).astype(LOW)
            raised_ref[0, pair * 2 + half] = raised
            left = jnp.concatenate(
                [v2t[HD * half : HD * half + HD], jnp.ones((16, LONG), LOW)], axis=0
            )
            mixed = dot(left, raised, 1, 0)
            inverse = 1.0 / mixed[HD : HD + 1]
            contexts.append(mixed[:HD] * inverse)
            inverses.append(jnp.broadcast_to(inverse, (HD, LONG)))
        context = jnp.concatenate(contexts, axis=0)
        ctxt_ref[pair * PAIR : pair * PAIR + PAIR, :] = context.astype(LOW)
        ctx_ref[:, cols] = context.T.astype(LOW)
        inv_ref[:, cols] = jnp.concatenate(inverses, axis=0).T


def weight_cols(weights, rows, at):
    return pl.BlockSpec((weights.shape[0], rows, QUAD), lambda j, b, *_: (0, at, j))


def attend(kind, x, weights, rows, vec):
    count = x.shape[0]
    blocks = count // LONG
    tokens = pl.BlockSpec((LONG, QUAD), lambda j, b, *_: (b, j))
    act = jax.ShapeDtypeStruct((count, D), LOW)
    return pl.pallas_call(
        attend_kernel,
        grid_spec=pltpu.PrefetchScalarGridSpec(
            num_scalar_prefetch=1,
            grid=(D // QUAD, blocks),
            in_specs=[
                pl.BlockSpec((LONG, D), lambda j, b, *_: (b, 0)),
                weight_cols(weights, rows, 0),
                weight_cols(weights, rows, 1),
                weight_cols(weights, rows, 2),
                pl.BlockSpec((8, QUAD), lambda j, b, *_: (0, j)),
            ],
            out_specs=[
                tokens,
                tokens,
                tokens,
                tokens,
                pl.BlockSpec((QUAD, LONG), lambda j, b, *_: (j, b)),
                pl.BlockSpec((1, QUAD // HD, LONG, LONG), lambda j, b, *_: (b, j, 0, 0)),
                tokens,
            ],
        ),
        out_shape=[
            act,
            act,
            act,
            act,
            jax.ShapeDtypeStruct((D, count), LOW),
            jax.ShapeDtypeStruct((blocks, H, LONG, LONG), LOW),
            jax.ShapeDtypeStruct((count, D), WIDE),
        ],
        compiler_params=params(),
        cost_estimate=cost(6 * count * D * D + 8 * count * LONG * D, 30 << 20, count * LONG * H),
        name="attend",
    )(kind, x, weights, weights, weights, vec)


def attend_back_kernel(
    xt_ref,
    d_ref,
    ctx_ref,
    inv_ref,
    q_ref,
    k_ref,
    v_ref,
    raised_ref,
    dq_ref,
    dk_ref,
    dv_ref,
    grads_ref,
    bias_ref,
    totals,
):
    block = pl.program_id(1)
    halves = half_masks()
    minus = jnp.full((LONG, PAIR), -1.0, LOW)
    for pair in range(QUAD // PAIR):
        cols = pl.ds(pair * PAIR, PAIR)
        d2 = d_ref[:, cols].astype(WIDE) * inv_ref[:, cols] * HD ** (-0.5)
        along = d2 * ctx_ref[:, cols].astype(WIDE)
        q2 = q_ref[:, cols].astype(WIDE)
        k2t = k_ref[:, cols].T
        values = jnp.concatenate([v_ref[:, cols], minus], axis=1)
        dqt, dk, dv = [], 0, 0
        for half in range(2):
            dm = (d2 * halves[half]).astype(LOW)
            am = (along * halves[half]).astype(LOW)
            raised = raised_ref[0, pair * 2 + half]
            dp = dot(values, jnp.concatenate([dm, am], axis=1), 1, 1)
            ds = (raised.astype(WIDE) * dp).astype(LOW)
            dv = dv + dot(raised, dm, 1, 0)
            dk = dk + dot(ds, (q2 * halves[half]).astype(LOW), 1, 0)
            dqt.append(dot(k2t[HD * half : HD * half + HD], ds, 1, 0))
        dv_ref[:, cols] = (dv * HD**0.5).astype(LOW)
        dk_ref[:, cols] = dk.astype(LOW)
        dq_ref[:, cols] = jnp.concatenate(dqt, axis=0).T.astype(LOW)
    xt = xt_ref[...]
    for at, ref in enumerate((dq_ref, dk_ref, dv_ref)):
        grad = dot(xt, ref[...], 1, 0)

        @pl.when(block == 0)
        def _(grad=grad, at=at):
            totals[at] = grad

        @pl.when(block != 0)
        def _(grad=grad, at=at):
            totals[at] += grad

    @pl.when(block == pl.num_programs(1) - 1)
    def _():
        grads_ref[...] = totals[...].astype(LOW)

    sums = jnp.concatenate(
        [
            token_sum(dq_ref[...].astype(WIDE)),
            token_sum(dv_ref[...].astype(WIDE)),
            jnp.zeros((6, QUAD), WIDE),
        ],
        axis=0,
    )

    @pl.when(block == 0)
    def _():
        bias_ref[...] = sums

    @pl.when(block != 0)
    def _():
        bias_ref[...] += sums


def attend_back(xt, d, ctx, inv, q, k, v, raised):
    count = q.shape[0]
    tokens = pl.BlockSpec((LONG, QUAD), lambda j, b: (b, j))
    act = jax.ShapeDtypeStruct((count, D), LOW)
    return pl.pallas_call(
        attend_back_kernel,
        grid=(D // QUAD, count // LONG),
        in_specs=[pl.BlockSpec((D, LONG), lambda j, b: (0, b))]
        + [tokens] * 6
        + [pl.BlockSpec((1, QUAD // HD, LONG, LONG), lambda j, b: (b, j, 0, 0))],
        out_specs=[
            tokens,
            tokens,
            tokens,
            pl.BlockSpec((3, D, QUAD), lambda j, b: (0, 0, j)),
            pl.BlockSpec((8, QUAD), lambda j, b: (0, j)),
        ],
        out_shape=[
            act,
            act,
            act,
            jax.ShapeDtypeStruct((3, D, D), LOW),
            jax.ShapeDtypeStruct((8, D), WIDE),
        ],
        scratch_shapes=[pltpu.VMEM((3, D, QUAD), WIDE)],
        compiler_params=params(),
        cost_estimate=cost(6 * count * D * D + 16 * count * LONG * D, 30 << 20),
        name="attend_back",
    )(xt, d, ctx, inv, q, k, v, raised)


def up_kernel(
    ctx_ref, x_ref, wo_ref, vec_ref, wu_ref, bu_ref,
    act_ref, slope_ref, norm_ref, inv_ref, hlt_ref, hl_ref,
):
    count = ctx_ref.shape[0]
    step = 256

    @pl.when(pl.program_id(0) == 0)
    def _():
        bias = vec_ref[OUT_BIAS : OUT_BIAS + 1]
        gain = vec_ref[ATTN_GAIN : ATTN_GAIN + 1]
        shift = vec_ref[ATTN_SHIFT : ATTN_SHIFT + 1]
        wo = flat(wo_ref)
        for at in range(0, count, step):
            rows = pl.ds(at, step)
            total = x_ref[rows].astype(WIDE) + dot(ctx_ref[rows], wo, 1, 0) + bias
            centered = total - row_mean(total)
            inverse = lax.rsqrt(row_mean(centered * centered) + EPSILON)
            norm = centered * inverse
            norm_ref[rows] = norm
            inv_ref[rows] = jnp.broadcast_to(inverse, (step, 128))
            hidden = (norm * gain + shift).astype(LOW)
            hl_ref[rows] = hidden
            hlt_ref[:, rows] = hidden.T

    bias = bu_ref[...]
    weight = flat(wu_ref)
    for at in range(0, count, step):
        rows = pl.ds(at, step)
        before = dot(hl_ref[rows], weight, 1, 0) + bias
        half = 0.5 * (1.0 + lax.erf(before * 0.7071067811865476))
        act_ref[rows] = (before * half).astype(LOW)
        slope_ref[rows] = (
            half + before * jnp.exp(-0.5 * before * before) * 0.3989422804014327
        ).astype(LOW)


def up_call(ctx, x, second, rows, vec, up_bias):
    count = x.shape[0]
    hidden = up_bias.shape[1]
    cols = lambda r: pl.BlockSpec((r, TILE), lambda j: (0, j))
    return pl.pallas_call(
        up_kernel,
        grid=(hidden // TILE,),
        in_specs=[
            whole((count, D)),
            whole((count, D)),
            pl.BlockSpec(
                (second.shape[0], rows, D), lambda j: (0, 0, 0), pipeline_mode=pl.Buffered(1)
            ),
            whole((8, D)),
            pl.BlockSpec((second.shape[0], rows, D), lambda j: (0, 1 + j, 0)),
            cols(1),
        ],
        out_specs=[
            cols(count),
            cols(count),
            whole((count, D)),
            whole((count, 128)),
            whole((D, count)),
        ],
        out_shape=[
            jax.ShapeDtypeStruct((count, hidden), LOW),
            jax.ShapeDtypeStruct((count, hidden), LOW),
            jax.ShapeDtypeStruct((count, D), WIDE),
            jax.ShapeDtypeStruct((count, 128), WIDE),
            jax.ShapeDtypeStruct((D, count), LOW),
        ],
        scratch_shapes=[pltpu.VMEM((count, D), LOW)],
        compiler_params=params(),
        cost_estimate=cost(2 * count * D * (D + hidden), 30 << 20, 2 * count * hidden),
        name="up",
    )(ctx, x, second, vec, second, up_bias)


def down_kernel(
    act_ref, wd_ref, norm_ref, vec_ref, cot_ref, out_ref, grad_ref, low_ref, sums_ref
):
    row = lambda at: vec_ref[at : at + 1]
    total = (
        norm_ref[...] * row(ATTN_GAIN)
        + row(ATTN_SHIFT)
        + (dot(act_ref[...], flat(wd_ref), 1, 0) + row(DOWN_BIAS))
    )
    centered = total - row_mean(total)
    inverse = lax.rsqrt(row_mean(centered * centered) + EPSILON)
    norm = centered * inverse
    out_ref[...] = (norm * row(FFN_GAIN) + row(FFN_SHIFT)).astype(LOW)
    grad_out = cot_ref[...].astype(WIDE)
    scaled = grad_out * row(FFN_GAIN)
    grad = inverse * (scaled - row_mean(scaled) - norm * row_mean(scaled * norm))
    grad_ref[...] = grad
    low = grad.astype(LOW)
    low_ref[...] = low
    sums = jnp.concatenate(
        [
            token_sum(grad_out * norm),
            token_sum(grad_out),
            token_sum(low.astype(WIDE)),
            jnp.zeros((5, D), WIDE),
        ],
        axis=0,
    )

    @pl.when(pl.program_id(0) == 0)
    def _():
        sums_ref[...] = sums

    @pl.when(pl.program_id(0) != 0)
    def _():
        sums_ref[...] += sums


def down_call(act, third, norm, vec, cotangent):
    count, hidden = act.shape
    tile = 256
    rows = lambda c: pl.BlockSpec((tile, c), lambda i: (i, 0))
    return pl.pallas_call(
        down_kernel,
        grid=(count // tile,),
        in_specs=[rows(hidden), whole(third.shape), rows(D), whole((8, D)), rows(D)],
        out_specs=[rows(D), rows(D), rows(D), whole((8, D))],
        out_shape=[
            jax.ShapeDtypeStruct((count, D), LOW),
            jax.ShapeDtypeStruct((count, D), WIDE),
            jax.ShapeDtypeStruct((count, D), LOW),
            jax.ShapeDtypeStruct((8, D), WIDE),
        ],
        compiler_params=params(),
        cost_estimate=cost(2 * count * D * hidden, 25 << 20),
        name="down",
    )(act, third, norm, vec, cotangent)


def down_grad_kernel(act_ref, low_ref, grad_ref):
    grad_ref[...] = dot(act_ref[...], low_ref[...], 0, 0).astype(LOW)


def down_grad_call(act, low):
    count, hidden = act.shape
    return pl.pallas_call(
        down_grad_kernel,
        grid=(hidden // TILE,),
        in_specs=[pl.BlockSpec((count, TILE), lambda j: (0, j)), whole((count, D))],
        out_specs=pl.BlockSpec((TILE, D), lambda j: (j, 0)),
        out_shape=jax.ShapeDtypeStruct((hidden, D), LOW),
        compiler_params=params(),
        cost_estimate=cost(2 * count * D * hidden, 15 << 20),
        name="down_grad",
    )(act, low)


def up_grad_kernel(
    low_ref, wd_ref, slope_ref, hlt_ref, wu_ref, grad_ref,
    up_ref, bias_ref, hidden_ref, before_scr,
):
    step = pl.program_id(0)
    before_scr[...] = (dot(low_ref[...], flat(wd_ref), 1, 1) * slope_ref[...].astype(WIDE)).astype(
        LOW
    )
    before = before_scr[...]
    up_ref[0] = dot(hlt_ref[...], before, 1, 0).astype(LOW)
    bias_ref[...] = token_sum(before.astype(WIDE))
    back = dot(before, flat(wu_ref), 1, 1)

    @pl.when(step == 0)
    def _():
        hidden_ref[...] = back + grad_ref[...]

    @pl.when(step != 0)
    def _():
        hidden_ref[...] += back


def up_grad_call(low, third, slope, hlt, second, rows, grad):
    count, hidden = slope.shape
    steps = hidden // TILE
    cols = lambda r: pl.BlockSpec((r, TILE), lambda j: (0, j))
    return pl.pallas_call(
        up_grad_kernel,
        grid=(steps,),
        in_specs=[
            whole((count, D)),
            pl.BlockSpec((third.shape[0] // steps,) + third.shape[1:], lambda j: (j, 0, 0)),
            cols(count),
            whole((D, count)),
            pl.BlockSpec((second.shape[0], rows, D), lambda j: (0, 1 + j, 0)),
            whole((count, D)),
        ],
        out_specs=[
            pl.BlockSpec((1, D, TILE), lambda j: (j, 0, 0)),
            cols(1),
            whole((count, D)),
        ],
        out_shape=[
            jax.ShapeDtypeStruct((steps, D, TILE), LOW),
            jax.ShapeDtypeStruct((1, hidden), WIDE),
            jax.ShapeDtypeStruct((count, D), WIDE),
        ],
        scratch_shapes=[pltpu.VMEM((count, TILE), LOW)],
        compiler_params=params(),
        cost_estimate=cost(6 * count * D * hidden, 40 << 20),
        name="up_grad",
    )(low, third, slope, hlt, second, grad)


def norm_back_kernel(
    hidden_ref, norm_ref, inv_ref, vec_ref, ctxt_ref, wo_ref,
    grad_ref, out_ref, ctx_ref, sums_ref, low_scr,
):
    count = hidden_ref.shape[0]
    step = 256
    gain = vec_ref[ATTN_GAIN : ATTN_GAIN + 1]
    wo = flat(wo_ref)
    sums = 0
    for at in range(0, count, step):
        rows = pl.ds(at, step)
        hidden = hidden_ref[rows]
        norm = norm_ref[rows]
        scaled = hidden * gain
        grad = inv_ref[rows][:, 0:1] * (
            scaled - row_mean(scaled) - norm * row_mean(scaled * norm)
        )
        grad_ref[rows] = grad
        low = grad.astype(LOW)
        low_scr[rows] = low
        sums = sums + jnp.concatenate(
            [
                token_sum(hidden * norm),
                token_sum(hidden),
                token_sum(low.astype(WIDE)),
                jnp.zeros((5, D), WIDE),
            ],
            axis=0,
        )
        ctx_ref[rows] = dot(low, wo, 1, 1).astype(LOW)
    sums_ref[...] = sums
    out_ref[0] = dot(ctxt_ref[...], low_scr[...], 1, 0).astype(LOW)


def norm_back_call(hidden, norm, inv, vec, ctxt, second, rows):
    count = hidden.shape[0]
    return pl.pallas_call(
        norm_back_kernel,
        grid=(1,),
        in_specs=[
            whole((count, D)),
            whole((count, D)),
            whole((count, 128)),
            whole((8, D)),
            whole((D, count)),
            whole((second.shape[0], rows, D)),
        ],
        out_specs=[whole((count, D)), whole((1, D, D)), whole((count, D)), whole((8, D))],
        out_shape=[
            jax.ShapeDtypeStruct((count, D), WIDE),
            jax.ShapeDtypeStruct((1, D, D), LOW),
            jax.ShapeDtypeStruct((count, D), LOW),
            jax.ShapeDtypeStruct((8, D), WIDE),
        ],
        scratch_shapes=[pltpu.VMEM((count, D), LOW)],
        compiler_params=params(),
        cost_estimate=cost(4 * count * D * D, 20 << 20),
        name="norm_back",
    )(hidden, norm, inv, vec, ctxt, second)


def input_grad_kernel(dq_ref, dk_ref, dv_ref, wq_ref, wk_ref, wv_ref, grad_ref, out_ref):
    out_ref[...] = (
        dot(dq_ref[...], flat(wq_ref), 1, 1)
        + dot(dk_ref[...], flat(wk_ref), 1, 1)
        + dot(dv_ref[...], flat(wv_ref), 1, 1)
        + grad_ref[...]
    )


def input_grad_call(dq, dk, dv, first, rows, grad):
    count = dq.shape[0]
    tile = 512
    tokens = pl.BlockSpec((tile, D), lambda i: (i, 0))

    def weight(at):
        return pl.BlockSpec(
            (first.shape[0], rows, D), lambda i: (0, at, 0), pipeline_mode=pl.Buffered(1)
        )

    return pl.pallas_call(
        input_grad_kernel,
        grid=(count // tile,),
        in_specs=[tokens] * 3 + [weight(0), weight(1), weight(2), tokens],
        out_specs=tokens,
        out_shape=jax.ShapeDtypeStruct((count, D), WIDE),
        compiler_params=params(),
        cost_estimate=cost(6 * count * D * D, 15 << 20),
        name="input_grad",
    )(dq, dk, dv, first, first, first, grad)


def swap(value, mask, count):
    return lax.ppermute(value, "fsdp", [(i, i ^ mask) for i in range(count)])


def gather_rows(piece, count):
    me = lax.axis_index("fsdp")
    held = piece[None]
    bit = count // 2
    while bit:
        other = swap(held, bit, count)
        mine_low = (me & bit) == 0
        held = jnp.stack(
            [jnp.where(mine_low, held, other), jnp.where(mine_low, other, held)], axis=1
        ).reshape((-1,) + piece.shape)
        bit //= 2
    return held


def pick(parts, at):
    picked = []
    for part in parts:
        k, count, rows, width = part.shape
        pairs = part.reshape(k, count // 2, 2, rows, width)
        half = lax.dynamic_index_in_dim(pairs, at, 2, keepdims=False)
        picked.append(jnp.moveaxis(half, 0, 1).reshape(count // 2, k * rows, width))
    return picked[0] if len(picked) == 1 else jnp.concatenate(picked, axis=1)


def scatter_sum(parts, count):
    me = lax.axis_index("fsdp")
    held = parts
    bit = 1
    while bit < count:
        mine = ((me & bit) != 0).astype(jnp.int32)
        other = swap(pick(held, 1 - mine), bit, count)
        total = (pick(held, mine).astype(WIDE) + other.astype(WIDE)).astype(LOW)
        held = [total[None]]
        bit *= 2
    held = held[0][0, 0]
    other = lax.ppermute(held, "rep", [(0, 1), (1, 0)])
    return held.astype(WIDE) + other.astype(WIDE)


def matrices(gathered, number, rows):
    if rows % 16 == 0:
        return gathered, rows
    count = gathered.shape[0]
    parts = gathered[:, : number * rows].reshape(count, number, rows, D)
    return jnp.moveaxis(parts, 1, 0).reshape(1, number * count * rows, D), count * rows


def shards(
    inputs,
    block_kind,
    query_weight,
    query_bias,
    key_weight,
    value_weight,
    value_bias,
    out_weight,
    out_bias,
    attn_gain,
    attn_shift,
    up_weight,
    up_bias,
    down_weight,
    down_bias,
    ffn_gain,
    ffn_shift,
    cotangent,
):
    rows = query_weight.shape[0]
    count = D // rows
    hidden = up_weight.shape[1]
    steps = hidden // TILE
    vectors = (
        query_bias,
        value_bias,
        out_bias,
        attn_gain,
        attn_shift,
        down_bias,
        ffn_gain,
        ffn_shift,
    )
    used = 8 * rows + up_bias.shape[0]
    spare = -(-used // D)
    packed = jnp.concatenate(vectors + (up_bias, jnp.zeros((spare * D - used,), LOW)))
    first = gather_rows(
        jnp.concatenate([query_weight, key_weight, value_weight, packed.reshape(spare, D)]), count
    )
    second = gather_rows(
        jnp.concatenate(
            [out_weight] + [up_weight[:, TILE * i : TILE * (i + 1)] for i in range(steps)]
        ),
        count,
    )
    third = gather_rows(down_weight, count)
    whole_packed = first[:, 3 * rows :].reshape(count, spare * D)
    vec = (
        jnp.moveaxis(whole_packed[:, : 8 * rows].reshape(count, 8, rows), 1, 0)
        .reshape(8, D)
        .astype(WIDE)
    )
    all_up_bias = whole_packed[:, 8 * rows : used].reshape(1, hidden).astype(WIDE)
    first, block = matrices(first, 3, rows)
    second, _ = matrices(second, 1 + steps, rows)

    q, k, v, ctx, ctxt, raised, inv = attend(block_kind, inputs, first, block, vec)
    act, slope, norm, first_inv, hlt = up_call(ctx, inputs, second, block, vec, all_up_bias)
    layer_out, grad, low, ffn_sums = down_call(act, third, norm, vec, cotangent)
    down_grad = down_grad_call(act, low)
    up_grad, up_bias_grad, grad_hidden = up_grad_call(low, third, slope, hlt, second, block, grad)
    grad_attn, out_grad, grad_ctx, attn_sums = norm_back_call(
        grad_hidden, norm, first_inv, vec, ctxt, second, block
    )
    dq, dk, dv, qkv_grad, bias_sums = attend_back(
        inputs.T, grad_ctx, ctx, inv, q, k, v, raised
    )
    input_grad = input_grad_call(dq, dk, dv, first, block, grad_attn)

    sum_down = scatter_sum([down_grad.reshape(1, count, -1, D)], count)
    sum_second = scatter_sum(
        [out_grad.reshape(1, count, rows, D), up_grad.reshape(steps, count, rows, TILE)], count
    )
    vector_grads = jnp.concatenate([bias_sums[:2], attn_sums[2:3], attn_sums[:2], ffn_sums[2:3], ffn_sums[:2]])
    packed_grads = jnp.concatenate(
        [
            jnp.moveaxis(vector_grads.reshape(8, count, rows), 0, 1).reshape(count, 8 * rows),
            up_bias_grad.reshape(count, -1),
            jnp.zeros((count, spare * D - used), WIDE),
        ],
        axis=1,
    ).astype(LOW)
    sum_first = scatter_sum(
        [qkv_grad.reshape(3, count, rows, D), packed_grads.reshape(1, count, spare, D)], count
    )
    own = sum_first[3 * rows :].reshape(-1)
    vector = lambda at: own[at * rows : (at + 1) * rows]
    sum_up = jnp.concatenate(
        [sum_second[rows * (1 + i) : rows * (2 + i)] for i in range(steps)], axis=1
    )
    return (
        layer_out,
        input_grad,
        sum_first[:rows],
        vector(QUERY_BIAS),
        sum_first[rows : 2 * rows],
        sum_first[2 * rows : 3 * rows],
        vector(VALUE_BIAS),
        sum_second[:rows],
        vector(OUT_BIAS),
        vector(ATTN_GAIN),
        vector(ATTN_SHIFT),
        sum_up,
        own[8 * rows : used],
        sum_down,
        vector(DOWN_BIAS),
        vector(FFN_GAIN),
        vector(FFN_SHIFT),
    )


def solution(mesh):
    tokens = P(("rep", "fsdp"), None)
    matrix = P("fsdp", None)
    vector = P("fsdp")
    params_placed = (
        matrix,
        vector,
        matrix,
        matrix,
        vector,
        matrix,
        vector,
        vector,
        vector,
        matrix,
        vector,
        matrix,
        vector,
        vector,
        vector,
    )
    return jax.shard_map(
        shards,
        mesh=mesh,
        in_specs=(tokens, P(("rep", "fsdp")), *params_placed, tokens),
        out_specs=(tokens, tokens, *params_placed),
        check_vma=False,
    )
```

time: 622 us -> 444 us (0.71)
  matrix products: 244 us -> 0 us
  Pallas kernels: 0 us -> 131 us
  local copies, waits for them, and re-layouts: 103 us -> 51.4 us
  other arithmetic: 53.2 us -> 39.6 us
    dot_general x32 -> x0, matrix products: 244 us -> none  [the longest x6 53.8 us: project(): return jnp.dot(left, right, preferred_element_type=jnp.float32)]
    pallas_call x0 -> x8, Pallas kernels: none -> 131 us  [the longest x1 30.9 us: attend_back(): pl.pallas_call(attend_back_kernel, grid=(D // QUAD, count // LONG), in_sp...]
    unnamed x148 -> x36, local copies, waits for them, and re-layouts: 34.5 us -> 9.95 us
    reduce_sum x10 -> x0, other arithmetic: 15 us -> none  [the longest x2 5.12 us: attend_block(): total = jnp.sum(raised, axis=-1, keepdims=True)]
    reshape x14 -> x3, local copies, waits for them, and re-layouts: 11.8 us -> 0.12 us  [the longest x2 0.11 us: shards(): vector_grads.reshape(8, count, rows)]
    while x13 -> x0, local copies, waits for them, and re-layouts: 10.6 us -> none  [the longest x4 7.7 us: layer_forward(): lax.map(attend_block, (heads_view(query), heads_view(keys), heads_view(va...]
    squeeze x13 -> x0, local copies, waits for them, and re-layouts: 9.03 us -> none  [scatter_sum(): send = lax.dynamic_index_in_dim(pairs, 1 - mine, 1, keepdims=False)]
    convert_element_type x14 -> x4, local copies, waits for them, and re-layouts: 10.1 us -> 1.47 us  [the longest x3 0.79 us: shards(): vec = jnp.moveaxis(whole_packed[:, :8 * rows].reshape(count, 8, rows), 1,...]
  transfers between devices with their start and end apart: 27 -> 27, of which waited for: 14 -> 15; matrix products, arithmetic and copies ran while one was open for 22% -> 16% of each run, Pallas kernels for 0% -> 7%
where the time goes in v2:
time: 444 us; the launch traced here: 439 us
  waiting for transfers between devices  184 us (41%)
  Pallas kernels  131 us (30%)
  local copies, waits for them, and re-layouts  51.4 us (12%)
  other arithmetic  39.6 us (9%)
  starting transfers between devices  31 us (7%)
    ppermute x24, waiting for transfers between devices, swap(): return lax.ppermute(value, 'fsdp', [(i, i ^ mask) for i in range(count)])  178 us
    pallas_call x1, Pallas kernels, attend_back(): pl.pallas_call(attend_back_kernel, grid=(D // QUAD, count // LONG), in_sp...  30.9 us
    ppermute x24, starting transfers between devices, swap(): return lax.ppermute(value, 'fsdp', [(i, i ^ mask) for i in range(count)])  26.3 us
    pallas_call x1, Pallas kernels, up_grad_call(): pl.pallas_call(up_grad_kernel, grid=(steps,), in_specs=[whole((count, D))...  23.2 us
    pallas_call x1, Pallas kernels, attend(): pl.pallas_call(attend_kernel, grid_spec=pltpu.PrefetchScalarGridSpec(num_...  21.7 us
    another operation x21, other arithmetic, gather_rows(): jnp.stack([jnp.where(mine_low, held, other), jnp.where(mine_low, other, h...  17.4 us
    pallas_call x1, Pallas kernels, up_call(): pl.pallas_call(up_kernel, grid=(hidden // TILE,), in_specs=[whole((count,...  15.2 us
    convert_element_type x9, other arithmetic, scatter_sum(): total = (pick(held, mine).astype(WIDE) + other.astype(WIDE)).astype(LOW)  15.2 us
  transfers between devices with their start and end apart: 27, of which 15 were waited for; matrix products, arithmetic and copies ran while one was open for 16% of the time, Pallas kernels for 7%

profile of v2, /device:TPU:0, one launch (start us, length us, event | category | flops | bytes accessed | tf_op | source)
XLA Modules:
  0.0 438.9 jit_solution(17438278717026395145)
XLA Ops:
  0.7 4.1 collective-permute-start.8
  4.8 6.1 %concatenate.43 = bf16[768]{0:T(1024)(128)(2,1)S(1)} concatenate(bf16[48]{0:T(256)(128)(2,1)} %param.21, bf16[48]{0:T(256)(128)(2,1)} %param.24, bf16[48]{0:T(256)(128)(2,1)} %param.26, bf16[48]{0:T(256)(128)(2,1)} %param.27, bf16[48]{0:T(256)(128)(2,1)} %param.28, bf16[48]{0:T(256)(128)(2,1)} %param.32, bf16[48]{0:T(256)(128)(2,1)} %param.33, bf16[48]{0:T(256)(128)(2,1)} %param.34, ...), dimensions={0} | concatenate | bytes 3072 | tf_op jit(solution)/shard_map/concatenate | solution.py:650
  16.4 2.9 collective-permute-start.4
  19.3 17.8 %collective-permute-done = bf16[1,145,768]{2,1,0:T(8,128)(2,1)S(1)} collective-permute-done((bf16[1,145,768]{2,1,0:T(8,128)(2,1)S(1)}, bf16[1,145,768]{2,1,0:T(8,128)(2,1)S(1)}, u32[]{:S(2)}, u32[]{:S(2)}) %collective-permute-start) | collective-permute-done | bytes 222752 | tf_op jit(solution)/shard_map/ppermute | solution.py:564
  38.4 2.1 collective-permute-start.9
  40.4 3.8 collective-permute-done.4
  45.1 9.1 %collective-permute-done.1 = bf16[2,145,768]{2,1,0:T(8,128)(2,1)S(1)} collective-permute-done((bf16[2,145,768]{2,1,0:T(8,128)(2,1)S(1)}, bf16[2,145,768]{2,1,0:T(8,128)(2,1)S(1)}, u32[]{:S(2)}, u32[]{:S(2)}) %collective-permute-start.1) | collective-permute-done | bytes 445472 | tf_op jit(solution)/shard_map/ppermute | solution.py:564
  57.2 9.7 %collective-permute-done.9 = bf16[2,192,768]{2,1,0:T(8,128)(2,1)S(1)} collective-permute-done((bf16[2,192,768]{2,1,0:T(8,128)(2,1)S(1)}, bf16[2,192,768]{2,1,0:T(8,128)(2,1)S(1)}, u32[]{:S(2)}, u32[]{:S(2)}) %collective-permute-start.9) | collective-permute-done | bytes 589856 | tf_op jit(solution)/shard_map/ppermute | solution.py:564
  69.6 13.0 %collective-permute-done.5 = bf16[2,240,768]{2,1,0:T(8,128)(2,1)S(1)} collective-permute-done((bf16[2,240,768]{2,1,0:T(8,128)(2,1)S(1)}, bf16[2,240,768]{2,1,0:T(8,128)(2,1)S(1)}, u32[]{:S(2)}, u32[]{:S(2)}) %collective-permute-start.5) | collective-permute-done | bytes 737312 | tf_op jit(solution)/shard_map/ppermute | solution.py:564
  82.8 1.6 collective-permute-start.6
  87.7 16.2 %collective-permute-done.10 = bf16[4,192,768]{2,1,0:T(8,128)(2,1)} collective-permute-done((bf16[4,192,768]{2,1,0:T(8,128)(2,1)}, bf16[4,192,768]{2,1,0:T(8,128)(2,1)}, u32[]{:S(2)}, u32[]{:S(2)}) %collective-permute-start.10) | collective-permute-done | bytes 1179680 | tf_op jit(solution)/shard_map/ppermute | solution.py:564
  103.9 1.8 select_bitcast_fusion.9
  105.9 1.6 copy.96
  107.5 26.9 %collective-permute-done.6 = bf16[4,240,768]{2,1,0:T(8,128)(2,1)} collective-permute-done((bf16[4,240,768]{2,1,0:T(8,128)(2,1)S(1)}, bf16[4,240,768]{2,1,0:T(8,128)(2,1)}, u32[]{:S(2)}, u32[]{:S(2)}) %collective-permute-start.6) | collective-permute-done | bytes 1474592 | tf_op jit(solution)/shard_map/ppermute | solution.py:564
  136.3 1.8 copy.93
  138.3 1.8 copy.98
  140.2 2.2 select_bitcast_fusion.5
  143.0 1.8 copy-done
  146.3 21.7 %attend.1 = (bf16[1024,768]{1,0:T(8,128)(2,1)}, bf16[1024,768]{1,0:T(8,128)(2,1)}, bf16[1024,768]{1,0:T(8,128)(2,1)}, bf16[1024,768]{1,0:T(8,128)(2,1)}, bf16[76...) custom-call(s32[2]{0:T(128)} %kind_ref.1, bf16[1024,768]{1,0:T(8,128)(2,1)} %x_ref.3, ...), custom_call_target="tpu_custom_call" | custom-call | flops 6845104128 | bytes 31457280 | tf_op jit(solution)/shard_map/attend/pallas_call | solution.py:124
  168.0 2.7 select_bitcast_fusion.3
  171.2 2.5 copy.97
  173.7 3.1 select_bitcast_fusion.1
  177.3 3.0 copy.94
  180.3 15.2 %up.1 = (bf16[1024,3072]{1,0:T(8,128)(2,1)}, bf16[1024,3072]{1,0:T(8,128)(2,1)}, f32[1024,768]{1,0:T(8,128)}, f32[1024,128]{1,0:T(8,128)}, bf16[768,1024]{1,0:T(8,128)(2,1)}) custom-call(bf16[1024,768]{1,0:T(8,128)(2,1)} %get-tuple-element.45.ctx_ref, bf16[1024,768]{1,0:T(8,128)(2,1)} %x_ref.3, bf16[16,240,768]{2,1,0:T(8,128)(2,1)} %bitcast.225, ...), custom_call_target="tpu_custom_call" | custom-call | flops 6039797760 | bytes 31457280 | tf_op jit(solution)/shard_map/up/pallas_call | solution.py:306
  195.5 13.3 %down.1 = (bf16[1024,768]{1,0:T(8,128)(2,1)}, f32[1024,768]{1,0:T(8,128)}, bf16[1024,768]{1,0:T(8,128)(2,1)}, f32[8,768]{1,0:T(8,128)}) custom-call(bf16[1024,3072]{1,0:T(8,128)(2,1)} %get-tuple-element.46.act_ref, bf16[16,192,768]{2,1,0:T(8,128)(2,1)} %bitcast.249, f32[1024,768]{1,0:T(8,128)} %get-tuple-element.47.norm_ref, f32[8,768]{1,0:T(8,128)} %reshape.240.vec_ref, ...), custom_call_target="tpu_custom_call" | custom-call | flops 4831838208 | bytes 26214400 | tf_op jit(solution)/shard_map/down/pallas_call | solution.py:382
  208.8 9.2 %down_grad.1 = bf16[3072,768]{1,0:T(8,128)(2,1)} custom-call(bf16[1024,3072]{1,0:T(8,128)(2,1)} %get-tuple-element.46.act_ref, bf16[1024,768]{1,0:T(8,128)(2,1)} %get-tuple-element.49.low_ref), custom_call_target="tpu_custom_call" | custom-call | flops 4831838208 | bytes 15728640 | tf_op jit(solution)/shard_map/down_grad/pallas_call | solution.py:405
  218.0 23.2 %up_grad.1 = (bf16[4,768,768]{2,1,0:T(8,128)(2,1)}, f32[1,3072]{1,0:T(1,128)}, f32[1024,768]{1,0:T(8,128)}) custom-call(bf16[1024,768]{1,0:T(8,128)(2,1)} %get-tuple-element.49.low_ref, bf16[16,192,768]{2,1,0:T(8,128)(2,1)} %bitcast.250, bf16[1024,3072]{1,0:T(8,128)(2,1)} %get-tuple-element.50.slope_ref, bf16[768,1024]{1,0:T(8,128)(2,1)} %get-tuple-element.51.hlt_ref, ...), custom_call_target="tpu_custom_call" | custom-call | flops 14495514624 | bytes 41943040 | tf_op jit(solution)/shard_map/up_grad/pallas_call | solution.py:443
  241.2 9.1 %norm_back.1 = (f32[1024,768]{1,0:T(8,128)}, bf16[1,768,768]{2,1,0:T(8,128)(2,1)}, bf16[1024,768]{1,0:T(8,128)(2,1)}, f32[8,768]{1,0:T(8,128)}) custom-call(f32[1024,768]{1,0:T(8,128)} %get-tuple-element.53.hidden_ref, f32[1024,768]{1,0:T(8,128)} %get-tuple-element.47.norm_ref, f32[1024,128]{1,0:T(8,128)} %get-tuple-element.54.inv_ref, ...), custom_call_target="tpu_custom_call" | custom-call | flops 2415919104 | bytes 20971520 | tf_op jit(solution)/shard_map/norm_back/pallas_call | solution.py:507
  251.0 30.9 %attend_back.1 = (bf16[1024,768]{1,0:T(8,128)(2,1)}, bf16[1024,768]{1,0:T(8,128)(2,1)}, bf16[1024,768]{1,0:T(8,128)(2,1)}, bf16[3,768,768]{2,1,0:T(8,128)(2,1)}, f32[8,768]{1,0:T(8,128)}) custom-call(bf16[768,1024]{1,0:T(8,128)(2,1)} %bitcast.256, bf16[1024,768]{1,0:T(8,128)(2,1)} %get-tuple-element.56.d_ref, bf16[1024,768]{1,0:T(8,128)(2,1)} %get-tuple-element.45.ctx_ref, ...), custom_call_target="tpu_custom_call" | custom-call | flops 10066329600 | bytes 31457280 | tf_op jit(solution)/shard_map/attend_back/pallas_call | solution.py:238
  282.0 3.6 constant_dynamic-slice_fusion.6
  289.5 3.4 dynamic-slice_bitcast_fusion
  294.8 1.8 pad_maximum_fusion.4
  298.5 2.0 add_convert_fusion.1
  304.8 2.9 fusion
  309.4 16.5 %collective-permute-done.13 = bf16[4,145,768]{2,0,1:T(4,128)(2,1)} collective-permute-done((bf16[4,145,768]{2,0,1:T(4,128)(2,1)}, bf16[4,145,768]{2,0,1:T(4,128)(2,1)}, u32[]{:S(2)}, u32[]{:S(2)}) %collective-permute-start.13) | collective-permute-done | bytes 890912 | tf_op jit(solution)/shard_map/ppermute | solution.py:564
  328.4 2.7 add_convert_fusion
  333.8 6.1 %collective-permute-done.14 = bf16[2,145,768]{2,1,0:T(8,128)(2,1)} collective-permute-done((bf16[2,145,768]{2,1,0:T(8,128)(2,1)}, bf16[2,145,768]{2,1,0:T(8,128)(2,1)}, u32[]{:S(2)}, u32[]{:S(2)}) %collective-permute-start.14) | collective-permute-done | bytes 445472 | tf_op jit(solution)/shard_map/ppermute | solution.py:564
  341.9 2.3 collective-permute-start.15
  344.3 9.4 %collective-permute-done.15 = bf16[1,145,768]{2,1,0:T(8,128)(2,1)} collective-permute-done((bf16[1,145,768]{2,1,0:T(8,128)(2,1)}, bf16[1,145,768]{2,1,0:T(8,128)(2,1)}, u32[]{:S(2)}, u32[]{:S(2)}) %collective-permute-start.15) | collective-permute-done | bytes 222752 | tf_op jit(solution)/shard_map/ppermute | solution.py:564
  356.2 1.9 fusion.2
  358.9 23.3 %collective-permute-done.18 = bf16[4,240,768]{2,1,0:T(8,128)(2,1)} collective-permute-done((bf16[4,240,768]{2,1,0:T(8,128)(2,1)}, bf16[4,240,768]{2,1,0:T(8,128)(2,1)}, u32[]{:S(2)}, u32[]{:S(2)}) %collective-permute-start.18) | collective-permute-done | bytes 1474592 | tf_op jit(solution)/shard_map/ppermute | solution.py:564
  382.2 1.7 fusion.1
  384.1 8.8 %input_grad.1 = f32[1024,768]{1,0:T(8,128)} custom-call(bf16[1024,768]{1,0:T(8,128)(2,1)} %get-tuple-element.62.dq_ref, bf16[1024,768]{1,0:T(8,128)(2,1)} %get-tuple-element.63.dk_ref, bf16[1024,768]{1,0:T(8,128)(2,1)} %get-tuple-element.64.dv_ref, bf16[16,145,768]{2,1,0:T(8,128)(2,1)} %bitcast.222, bf16[16,145,768]{2,1,0:T(8,128)(2,1)} %bitcast.223, ...), custom_call_target="tpu_custom_call" | custom-call | flops 3623878656 | bytes 15728640 | tf_op jit(solution)/shard_map/input_grad/pallas_call | solution.py:551
  394.7 4.1 collective-permute-start.25
  398.8 8.0 %collective-permute-done.19 = bf16[2,240,768]{2,1,0:T(8,128)(2,1)S(1)} collective-permute-done((bf16[2,240,768]{2,1,0:T(8,128)(2,1)S(1)}, bf16[2,240,768]{2,1,0:T(8,128)(2,1)S(1)}, u32[]{:S(2)}, u32[]{:S(2)}) %collective-permute-start.19) | collective-permute-done | bytes 737312 | tf_op jit(solution)/shard_map/ppermute | solution.py:564
  407.9 12.9 %collective-permute-done.25 = bf16[1,192,768]{2,1,0:T(8,128)(2,1)S(1)} collective-permute-done((bf16[1,192,768]{2,1,0:T(8,128)(2,1)S(1)}, bf16[1,192,768]{2,1,0:T(8,128)(2,1)S(1)}, u32[]{:S(2)}, u32[]{:S(2)}) %collective-permute-start.25) | collective-permute-done | bytes 294944 | tf_op jit(solution)/shard_map/ppermute | solution.py:564
  422.4 4.9 %collective-permute-done.20 = bf16[1,240,768]{2,1,0:T(8,128)(2,1)S(1)} collective-permute-done((bf16[1,240,768]{2,1,0:T(8,128)(2,1)S(1)}, bf16[1,240,768]{2,1,0:T(8,128)(2,1)S(1)}, u32[]{:S(2)}, u32[]{:S(2)}) %collective-permute-start.20) | collective-permute-done | bytes 368672 | tf_op jit(solution)/shard_map/ppermute | solution.py:564
  430.5 6.3 %collective-permute-done.21 = bf16[240,768]{1,0:T(8,128)(2,1)S(1)} collective-permute-done((bf16[240,768]{1,0:T(8,128)(2,1)S(1)}, bf16[240,768]{1,0:T(8,128)(2,1)S(1)}, u32[]{:S(2)}, u32[]{:S(2)}) %collective-permute-start.21) | collective-permute-done | bytes 368672 | tf_op jit(solution)/shard_map/ppermute | solution.py:602
  (154 shorter events, 56.7 us)
Async XLA Ops:
  0.7 37.6 %copy-start.7 = (bf16[192,768]{1,0:T(8,128)(2,1)S(1)}, bf16[192,768]{1,0:T(8,128)(2,1)}, u32[]{:S(2)}) copy-start(bf16[192,768]{1,0:T(8,128)(2,1)} %param.31) | copy-start | bytes 884740
  0.7 37.6 %collective-permute-start.8 = (bf16[1,192,768]{2,1,0:T(8,128)(2,1)}, bf16[1,192,768]{2,1,0:T(8,128)(2,1)S(1)}, u32[]{:S(2)}, u32[]{:S(2)}) collective-permute-start(bf16[1,192,768]{2,1,0:T(8,128)(2,1)} %bitcast.259), channel_id=1, source_target_pairs={{0,8},{1,9},{2,10},{3,11},{4,12},{5,13},{6,14},{7,15},{8,0},{9,1},... | collective-permute-start | bytes 884744 | tf_op jit(solution)/shard_map/ppermute | solution.py:564
  11.8 25.2 %collective-permute-start = (bf16[1,145,768]{2,1,0:T(8,128)(2,1)S(1)}, bf16[1,145,768]{2,1,0:T(8,128)(2,1)S(1)}, u32[]{:S(2)}, u32[]{:S(2)}) collective-permute-start(bf16[1,145,768]{2,1,0:T(8,128)(2,1)S(1)} %maximum_bitcast_fusion.3), channel_id=1, source_target_pairs={{0,8},{1,9},{2,10},{3,11},{4,12},{5,13},{6,14},{7,15},{8,0},{9,1},... | collective-permute-start | bytes 668168 | tf_op jit(solution)/shard_map/ppermute | solution.py:564
  16.4 27.8 %collective-permute-start.4 = (bf16[1,240,768]{2,1,0:T(8,128)(2,1)S(1)}, bf16[1,240,768]{2,1,0:T(8,128)(2,1)S(1)}, u32[]{:S(2)}, u32[]{:S(2)}) collective-permute-start(bf16[1,240,768]{2,1,0:T(8,128)(2,1)S(1)} %bitcast.258), channel_id=1, source_target_pairs={{0,8},{1,9},{2,10},{3,11},{4,12},{5,13},{6,14},{7,15},{8,0},{9,1},... | collective-permute-start | bytes 1105928 | tf_op jit(solution)/shard_map/ppermute | solution.py:564
  38.1 16.1 %collective-permute-start.1 = (bf16[2,145,768]{2,1,0:T(8,128)(2,1)S(1)}, bf16[2,145,768]{2,1,0:T(8,128)(2,1)S(1)}, u32[]{:S(2)}, u32[]{:S(2)}) collective-permute-start(bf16[2,145,768]{2,1,0:T(8,128)(2,1)S(1)} %maximum_bitcast_fusion.2), channel_id=1, source_target_pairs={{0,4},{1,5},{2,6},{3,7},{4,0},{5,1},{6,2},{7,3},{8,12},{9,13},{10,... | collective-permute-start | bytes 1336328 | tf_op jit(solution)/shard_map/ppermute | solution.py:564
  38.4 28.5 %collective-permute-start.9 = (bf16[2,192,768]{2,1,0:T(8,128)(2,1)S(1)}, bf16[2,192,768]{2,1,0:T(8,128)(2,1)S(1)}, u32[]{:S(2)}, u32[]{:S(2)}) collective-permute-start(bf16[2,192,768]{2,1,0:T(8,128)(2,1)S(1)} %maximum_bitcast_fusion.1), channel_id=1, source_target_pairs={{0,4},{1,5},{2,6},{3,7},{4,0},{5,1},{6,2},{7,3},{8,12},{9,13},{10,... | collective-permute-start | bytes 1769480 | tf_op jit(solution)/shard_map/ppermute | solution.py:564
  44.3 38.2 %collective-permute-start.5 = (bf16[2,240,768]{2,1,0:T(8,128)(2,1)S(1)}, bf16[2,240,768]{2,1,0:T(8,128)(2,1)S(1)}, u32[]{:S(2)}, u32[]{:S(2)}) collective-permute-start(bf16[2,240,768]{2,1,0:T(8,128)(2,1)S(1)} %maximum_bitcast_fusion), channel_id=1, source_target_pairs={{0,4},{1,5},{2,6},{3,7},{4,0},{5,1},{6,2},{7,3},{8,12},{9,13},{10,... | collective-permute-start | bytes 2211848 | tf_op jit(solution)/shard_map/ppermute | solution.py:564
  55.6 28.8 %collective-permute-start.2 = (bf16[4,145,768]{2,0,1:T(4,128)(2,1)}, bf16[4,145,768]{2,0,1:T(4,128)(2,1)}, u32[]{:S(2)}, u32[]{:S(2)}) collective-permute-start(bf16[4,145,768]{2,0,1:T(4,128)(2,1)} %copy.83), channel_id=1, source_target_pairs={{0,2},{1,3},{2,0},{3,1},{4,6},{5,7},{6,4},{7,5},{8,10},{9,11},{10,... | collective-permute-start | bytes 2672648 | tf_op jit(solution)/shard_map/ppermute | solution.py:564
  68.1 35.8 %collective-permute-start.10 = (bf16[4,192,768]{2,1,0:T(8,128)(2,1)}, bf16[4,192,768]{2,1,0:T(8,128)(2,1)}, u32[]{:S(2)}, u32[]{:S(2)}) collective-permute-start(bf16[4,192,768]{2,1,0:T(8,128)(2,1)} %bitcast.36), channel_id=1, source_target_pairs={{0,2},{1,3},{2,0},{3,1},{4,6},{5,7},{6,4},{7,5},{8,10},{9,11},{10,... | collective-permute-start | bytes 3538952 | tf_op jit(solution)/shard_map/ppermute | solution.py:564
  82.8 51.6 %collective-permute-start.6 = (bf16[4,240,768]{2,1,0:T(8,128)(2,1)S(1)}, bf16[4,240,768]{2,1,0:T(8,128)(2,1)}, u32[]{:S(2)}, u32[]{:S(2)}) collective-permute-start(bf16[4,240,768]{2,1,0:T(8,128)(2,1)S(1)} %bitcast.241), channel_id=1, source_target_pairs={{0,2},{1,3},{2,0},{3,1},{4,6},{5,7},{6,4},{7,5},{8,10},{9,11},{10,... | collective-permute-start | bytes 4423688 | tf_op jit(solution)/shard_map/ppermute | solution.py:564
  87.7 52.5 %collective-permute-start.3 = (bf16[8,145,768]{2,0,1:T(8,128)(2,1)}, bf16[8,145,768]{2,0,1:T(8,128)(2,1)}, u32[]{:S(2)}, u32[]{:S(2)}) collective-permute-start(bf16[8,145,768]{2,0,1:T(8,128)(2,1)} %copy.87), channel_id=1, source_target_pairs={{0,1},{1,0},{2,3},{3,2},{4,5},{5,4},{6,7},{7,6},{8,9},{9,8},{10,11... | collective-permute-start | bytes 5345288 | tf_op jit(solution)/shard_map/ppermute | solution.py:564
  107.5 60.5 %collective-permute-start.11 = (bf16[8,192,768]{2,1,0:T(8,128)(2,1)}, bf16[8,192,768]{2,1,0:T(8,128)(2,1)}, u32[]{:S(2)}, u32[]{:S(2)}) collective-permute-start(bf16[8,192,768]{2,1,0:T(8,128)(2,1)} %bitcast.39), channel_id=1, source_target_pairs={{0,1},{1,0},{2,3},{3,2},{4,5},{5,4},{6,7},{7,6},{8,9},{9,8},{10,11... | collective-permute-start | bytes 7077896 | tf_op jit(solution)/shard_map/ppermute | solution.py:564
  136.3 2.1 copy-start.5
  138.1 35.6 %collective-permute-start.7 = (bf16[8,240,768]{2,1,0:T(8,128)(2,1)}, bf16[8,240,768]{2,1,0:T(8,128)(2,1)}, u32[]{:S(2)}, u32[]{:S(2)}) collective-permute-start(bf16[8,240,768]{2,1,0:T(8,128)(2,1)} %bitcast.25), channel_id=1, source_target_pairs={{0,1},{1,0},{2,3},{3,2},{4,5},{5,4},{6,7},{7,6},{8,9},{9,8},{10,11... | collective-permute-start | bytes 8847368 | tf_op jit(solution)/shard_map/ppermute | solution.py:564
  142.9 1.8 copy-start
  241.1 9.8 %copy-start.11 = (f32[8,768]{1,0:T(8,128)S(1)}, f32[8,768]{1,0:T(8,128)}, u32[]{:S(2)}) copy-start(f32[8,768]{1,0:T(8,128)} %get-tuple-element.69) | copy-start | bytes 73732
  251.0 31.0 %copy-start.9 = (bf16[8,768]{1,0:T(8,128)(2,1)}, bf16[8,768]{1,0:T(8,128)(2,1)S(1)}, u32[]{:S(2)}) copy-start(bf16[8,768]{1,0:T(8,128)(2,1)S(1)} %convert.38) | copy-start | bytes 36868
  251.0 30.9 %copy-start.10 = (bf16[8,768]{1,0:T(8,128)(2,1)}, bf16[8,768]{1,0:T(8,128)(2,1)S(1)}, u32[]{:S(2)}) copy-start(bf16[8,768]{1,0:T(8,128)(2,1)S(1)} %convert.39) | copy-start | bytes 36868
  285.5 0.9 slice-start.2
  285.5 0.9 slice-start.3
  285.5 1.1 copy-start.12
  287.5 5.6 %slice-start = ((s8[4718592]{0:T(1024)(128)(4,1)}), s8[4194304]{0:T(1024)(128)(4,1)S(1)}, s32[]{:S(2)}) async-start(s8[4718592]{0:T(1024)(128)(4,1)} %bitcast.246), calls=%async_computation | async-start | bytes 8388608
  287.7 5.5 %slice-start.1 = ((s8[4718592]{0:T(1024)(128)(4,1)}), s8[524288]{0:T(1024)(128)(4,1)S(1)}, s32[]{:S(2)}) async-start(s8[4718592]{0:T(1024)(128)(4,1)} %bitcast.246), calls=%async_computation.1 | async-start | bytes 1048576
  289.2 9.2 %collective-permute-start.12 = (bf16[8,145,768]{2,0,1:T(8,128)(2,1)}, bf16[8,145,768]{2,0,1:T(8,128)(2,1)}, u32[]{:S(2)}, u32[]{:S(2)}) collective-permute-start(bf16[8,145,768]{2,0,1:T(8,128)(2,1)} %copy.104), channel_id=1, source_target_pairs={{0,1},{1,0},{2,3},{3,2},{4,5},{5,4},{6,7},{7,6},{8,9},{9,8},{10,11... | collective-permute-start | bytes 5345288 | tf_op jit(solution)/shard_map/ppermute | solution.py:564
  292.9 12.0 %collective-permute-start.22 = (bf16[8,192,768]{2,1,0:T(8,128)(2,1)}, bf16[8,192,768]{2,1,0:T(8,128)(2,1)}, u32[]{:S(2)}, u32[]{:S(2)}) collective-permute-start(bf16[8,192,768]{2,1,0:T(8,128)(2,1)} %dynamic-slice_bitcast_fusion), channel_id=1, source_target_pairs={{0,1},{1,0},{2,3},{3,2},{4,5},{5,4},{6,7},{7,6},{8,9},{9,8},{10,11... | collective-permute-start | bytes 7077896 | tf_op jit(solution)/shard_map/ppermute | solution.py:564
  293.5 1.3 copy-start.6
  296.6 1.8 copy-start.8
  296.6 31.6 %collective-permute-start.17 = (bf16[8,240,768]{2,1,0:T(8,128)(2,1)}, bf16[8,240,768]{2,1,0:T(8,128)(2,1)}, u32[]{:S(2)}, u32[]{:S(2)}) collective-permute-start(bf16[8,240,768]{2,1,0:T(8,128)(2,1)} %pad_maximum_fusion.4), channel_id=1, source_target_pairs={{0,1},{1,0},{2,3},{3,2},{4,5},{5,4},{6,7},{7,6},{8,9},{9,8},{10,11... | collective-permute-start | bytes 8847368 | tf_op jit(solution)/shard_map/ppermute | solution.py:564
  300.5 1.2 copy-start.2
  303.1 22.9 %collective-permute-start.13 = (bf16[4,145,768]{2,0,1:T(4,128)(2,1)}, bf16[4,145,768]{2,0,1:T(4,128)(2,1)}, u32[]{:S(2)}, u32[]{:S(2)}) collective-permute-start(bf16[4,145,768]{2,0,1:T(4,128)(2,1)} %bitcast.214), channel_id=1, source_target_pairs={{0,2},{1,3},{2,0},{3,1},{4,6},{5,7},{6,4},{7,5},{8,10},{9,11},{10,... | collective-permute-start | bytes 2672648 | tf_op jit(solution)/shard_map/ppermute | solution.py:564
  307.8 19.5 %copy-start.1 = (bf16[8,192,768]{2,1,0:T(8,128)(2,1)}, bf16[8,192,768]{2,1,0:T(8,128)(2,1)S(1)}, u32[]{:S(2)}) copy-start(bf16[8,192,768]{2,1,0:T(8,128)(2,1)S(1)} %fusion) | copy-start | bytes 7077892
  307.8 18.2 %copy-start.3 = (bf16[8,145,768]{2,1,0:T(8,128)(2,1)S(1)}, bf16[8,145,768]{2,1,0:T(8,128)(2,1)}, u32[]{:S(2)}) copy-start(bf16[8,145,768]{2,1,0:T(8,128)(2,1)} %copy-done.2) | copy-start | bytes 5345284
  309.0 47.3 %collective-permute-start.23 = (bf16[4,192,768]{2,1,0:T(8,128)(2,1)}, bf16[4,192,768]{2,1,0:T(8,128)(2,1)}, u32[]{:S(2)}, u32[]{:S(2)}) collective-permute-start(bf16[4,192,768]{2,1,0:T(8,128)(2,1)} %dynamic-slice_bitcast_fusion.2), channel_id=1, source_target_pairs={{0,2},{1,3},{2,0},{3,1},{4,6},{5,7},{6,4},{7,5},{8,10},{9,11},{10,... | collective-permute-start | bytes 3538952 | tf_op jit(solution)/shard_map/ppermute | solution.py:564
  327.3 1.1 copy-start.4
  328.2 11.7 %collective-permute-start.14 = (bf16[2,145,768]{2,1,0:T(8,128)(2,1)}, bf16[2,145,768]{2,1,0:T(8,128)(2,1)}, u32[]{:S(2)}, u32[]{:S(2)}) collective-permute-start(bf16[2,145,768]{2,1,0:T(8,128)(2,1)} %dynamic-slice_bitcast_fusion.7), channel_id=1, source_target_pairs={{0,4},{1,5},{2,6},{3,7},{4,0},{5,1},{6,2},{7,3},{8,12},{9,13},{10,... | collective-permute-start | bytes 1336328 | tf_op jit(solution)/shard_map/ppermute | solution.py:564
  332.3 49.9 %collective-permute-start.18 = (bf16[4,240,768]{2,1,0:T(8,128)(2,1)}, bf16[4,240,768]{2,1,0:T(8,128)(2,1)}, u32[]{:S(2)}, u32[]{:S(2)}) collective-permute-start(bf16[4,240,768]{2,1,0:T(8,128)(2,1)} %dynamic-slice_bitcast_fusion.1), channel_id=1, source_target_pairs={{0,2},{1,3},{2,0},{3,1},{4,6},{5,7},{6,4},{7,5},{8,10},{9,11},{10,... | collective-permute-start | bytes 4423688 | tf_op jit(solution)/shard_map/ppermute | solution.py:564
  341.9 11.7 %collective-permute-start.15 = (bf16[1,145,768]{2,1,0:T(8,128)(2,1)}, bf16[1,145,768]{2,1,0:T(8,128)(2,1)}, u32[]{:S(2)}, u32[]{:S(2)}) collective-permute-start(bf16[1,145,768]{2,1,0:T(8,128)(2,1)} %constant_dynamic-slice_fusion.4), channel_id=1, source_target_pairs={{0,8},{1,9},{2,10},{3,11},{4,12},{5,13},{6,14},{7,15},{8,0},{9,1},... | collective-permute-start | bytes 668168 | tf_op jit(solution)/shard_map/ppermute | solution.py:564
  354.6 38.2 %collective-permute-start.16 = (bf16[145,768]{1,0:T(8,128)(2,1)S(1)}, bf16[145,768]{1,0:T(8,128)(2,1)S(1)}, u32[]{:S(2)}, u32[]{:S(2)}) collective-permute-start(bf16[145,768]{1,0:T(8,128)(2,1)S(1)} %fusion.9), channel_id=1, source_target_pairs={{0,16},{16,0},{1,17},{17,1},{2,18},{18,2},{3,19},{19,3},{4,20},{20... | collective-permute-start | bytes 668168 | tf_op jit(solution)/shard_map/ppermute | solution.py:602
  358.2 35.3 %collective-permute-start.24 = (bf16[2,192,768]{2,1,0:T(8,128)(2,1)S(1)}, bf16[2,192,768]{2,1,0:T(8,128)(2,1)}, u32[]{:S(2)}, u32[]{:S(2)}) collective-permute-start(bf16[2,192,768]{2,1,0:T(8,128)(2,1)S(1)} %dynamic-slice_bitcast_fusion.4), channel_id=1, source_target_pairs={{0,4},{1,5},{2,6},{3,7},{4,0},{5,1},{6,2},{7,3},{8,12},{9,13},{10,... | collective-permute-start | bytes 1769480 | tf_op jit(solution)/shard_map/ppermute | solution.py:564
  384.0 22.8 %collective-permute-start.19 = (bf16[2,240,768]{2,1,0:T(8,128)(2,1)S(1)}, bf16[2,240,768]{2,1,0:T(8,128)(2,1)S(1)}, u32[]{:S(2)}, u32[]{:S(2)}) collective-permute-start(bf16[2,240,768]{2,1,0:T(8,128)(2,1)S(1)} %dynamic-slice_bitcast_fusion.3), channel_id=1, source_target_pairs={{0,4},{1,5},{2,6},{3,7},{4,0},{5,1},{6,2},{7,3},{8,12},{9,13},{10,... | collective-permute-start | bytes 2211848 | tf_op jit(solution)/shard_map/ppermute | solution.py:564
  394.7 26.1 %collective-permute-start.25 = (bf16[1,192,768]{2,1,0:T(8,128)(2,1)S(1)}, bf16[1,192,768]{2,1,0:T(8,128)(2,1)S(1)}, u32[]{:S(2)}, u32[]{:S(2)}) collective-permute-start(bf16[1,192,768]{2,1,0:T(8,128)(2,1)S(1)} %constant_dynamic-slice_fusion), channel_id=1, source_target_pairs={{0,8},{1,9},{2,10},{3,11},{4,12},{5,13},{6,14},{7,15},{8,0},{9,1},... | collective-permute-start | bytes 884744 | tf_op jit(solution)/shard_map/ppermute | solution.py:564
  407.1 20.3 %collective-permute-start.20 = (bf16[1,240,768]{2,1,0:T(8,128)(2,1)S(1)}, bf16[1,240,768]{2,1,0:T(8,128)(2,1)S(1)}, u32[]{:S(2)}, u32[]{:S(2)}) collective-permute-start(bf16[1,240,768]{2,1,0:T(8,128)(2,1)S(1)} %constant_dynamic-slice_fusion.1), channel_id=1, source_target_pairs={{0,8},{1,9},{2,10},{3,11},{4,12},{5,13},{6,14},{7,15},{8,0},{9,1},... | collective-permute-start | bytes 1105928 | tf_op jit(solution)/shard_map/ppermute | solution.py:564
  420.9 8.8 %collective-permute-start.26 = (bf16[192,768]{1,0:T(8,128)(2,1)S(1)}, bf16[192,768]{1,0:T(8,128)(2,1)S(1)}, u32[]{:S(2)}, u32[]{:S(2)}) collective-permute-start(bf16[192,768]{1,0:T(8,128)(2,1)S(1)} %fusion.8), channel_id=1, source_target_pairs={{0,16},{16,0},{1,17},{17,1},{2,18},{18,2},{3,19},{19,3},{4,20},{20... | collective-permute-start | bytes 884744 | tf_op jit(solution)/shard_map/ppermute | solution.py:602
  427.4 9.3 %collective-permute-start.21 = (bf16[240,768]{1,0:T(8,128)(2,1)S(1)}, bf16[240,768]{1,0:T(8,128)(2,1)S(1)}, u32[]{:S(2)}, u32[]{:S(2)}) collective-permute-start(bf16[240,768]{1,0:T(8,128)(2,1)S(1)} %fusion.7), channel_id=1, source_target_pairs={{0,16},{16,0},{1,17},{17,1},{2,18},{18,2},{3,19},{19,3},{4,20},{20... | collective-permute-start | bytes 1105928 | tf_op jit(solution)/shard_map/ppermute | solution.py:602
